TPU v7x, 512 devices: a whole 4x4x16 slice. The times are simulated.
512 devices in a mesh: tower: 2 (over z_hi), ctx: 128 (over z_lo, x, y), dp: 2 (over core).
Axes of the slice: x: 4, y: 4, z: 16 (z_hi: 2, z_lo: 8; z = z_hi * 8 + z_lo), core: 2. Of those that a mesh axis runs over, the one named last changes fastest.
Arguments:
- query_self: bfloat16 [2, 32768, 512], P('tower', ('dp', 'ctx')), parts along dimension 1, may hold values from -6 to 6
- key_self: bfloat16 [2, 32768, 512], P('tower', ('dp', 'ctx')), parts along dimension 1, may hold values from -6 to 6
- value_self: bfloat16 [2, 32768, 512], P('tower', ('dp', 'ctx')), parts along dimension 1, may hold values from -6 to 6
- query_cross: bfloat16 [2, 32768, 512], P('tower', ('dp', 'ctx')), parts along dimension 1, may hold values from -6 to 6
- key_cross: bfloat16 [2, 32768, 512], P('tower', ('dp', 'ctx')), parts along dimension 1, may hold values from -6 to 6
- value_cross: bfloat16 [2, 32768, 512], P('tower', ('dp', 'ctx')), parts along dimension 1, may hold values from -6 to 6
- cotangent: bfloat16 [2, 32768, 512], P('tower', ('dp', 'ctx')), parts along dimension 1, may hold values from -6 to 6
- block_slot: int32 [128], P('ctx'), may hold values from 0 to 127, as said below
Outputs:
- attended: bfloat16 [2, 32768, 512], P('tower', ('dp', 'ctx')), parts along dimension 1
- query_grad_self: bfloat16 [2, 32768, 512], P('tower', ('dp', 'ctx')), parts along dimension 1
- key_grad_self: bfloat16 [2, 32768, 512], P('tower', ('dp', 'ctx')), parts along dimension 1
- value_grad_self: bfloat16 [2, 32768, 512], P('tower', ('dp', 'ctx')), parts along dimension 1
- query_grad_cross: bfloat16 [2, 32768, 512], P('tower', ('dp', 'ctx')), parts along dimension 1
- key_grad_cross: bfloat16 [2, 32768, 512], P('tower', ('dp', 'ctx')), parts along dimension 1
- value_grad_cross: bfloat16 [2, 32768, 512], P('tower', ('dp', 'ctx')), parts along dimension 1
There are 2 independent parts, one for each index of `dp`. A program takes and returns all parts, laid end to end along the dimension named above; an argument that names none is the same for every part. Nothing has to cross between parts.
Inputs may be any that keep to these rules, and one draw needn't show every extreme that they name: `block_slot`: there is one offset c such that entry b is (b + c) modulo 128.
All inputs are finite; a program needn't handle non-finite values.
Results may differ from a plain program's by a relative error of at most 0.04.
Values may be sent and summed in bfloat16 or wider, within the bound.
No kernel may reach another device: no remote copies, remote signals or barrier semaphores. Data moves between devices by JAX's collectives and lax.ppermute only.
A program may use at most 64 MiB of HBM per device.

v0:
```python
import jax
import jax.numpy as jnp
from jax import lax
from jax.sharding import PartitionSpec as P

HEADS = 8
HEAD = 64


def swapped(value, axis, apart):
    mask = 2**apart
    pairs = [(source, source ^ mask) for source in range(lax.axis_size(axis))]
    return lax.ppermute(value, axis, pairs)


def passed_along(block, axis, distance):
    devices = range(lax.axis_size(axis))
    route = [((i - distance) % len(devices), i) for i in devices]
    return lax.ppermute(block, axis, route)


def as_sent(value):

    def short(part):
        return part.astype(jnp.bfloat16) if part.dtype == jnp.float32 else part

    return jax.tree.map(short, value)


def body(
    query_self, key_self, value_self, query_cross, key_cross, value_cross, cotangent, block_slot
):
    devices = lax.axis_size("ctx")
    group_size = min(8, devices // 2)
    query_s = query_self[0]
    query_c = query_cross[0]
    key_own = key_self[0]
    value_own = value_self[0]
    row_count, feature_count = query_s.shape
    score_scale = HEAD ** (-0.5)
    offsets = jnp.arange(row_count, dtype=jnp.int32)
    own_index = block_slot[0]
    upstream_heads = cotangent[0].reshape(row_count, HEADS, HEAD)
    partner_key, partner_value = swapped((key_cross[0], value_cross[0]), "tower", 0)

    def split_heads(matrix):
        return matrix.reshape(row_count, HEADS, HEAD)

    def masked_scores(query, keys, query_index, key_index):
        query_position = query_index * row_count + offsets
        key_position = key_index * row_count + offsets
        scores = (
            jnp.einsum(
                "ihd,jhd->hij",
                split_heads(query),
                split_heads(keys),
                preferred_element_type=jnp.float32,
            )
            * score_scale
        )
        return jnp.where((key_position[None, :] <= query_position[:, None])[None], scores, -1e30)

    def forward_tile(carried, query, keys, values, key_index):
        row_max, row_total, accumulated = carried
        scores = masked_scores(query, keys, own_index, key_index)
        new_max = jnp.maximum(row_max, jnp.max(scores, axis=2))
        factor = jnp.exp(row_max - new_max)
        weights = jnp.exp(scores - new_max[:, :, None])
        row_total = row_total * factor + jnp.sum(weights, axis=2)
        accumulated = accumulated * factor.T[:, :, None] + jnp.einsum(
            "hij,jhd->ihd",
            weights.astype(jnp.bfloat16),
            split_heads(values),
            preferred_element_type=jnp.float32,
        )
        return (new_max, row_total, accumulated)

    def forward_apply(carried, query, keys, values, key_index):
        return forward_tile(carried, query, keys, values, key_index)

    def tile_grads(query, upstream, keys, values, query_index, key_index, log_total, delta):
        scores = masked_scores(query, keys, query_index, key_index)
        probabilities = jnp.exp(scores - log_total[:, :, None])
        grad_probs = jnp.einsum(
            "ihd,jhd->hij", upstream, split_heads(values), preferred_element_type=jnp.float32
        )
        grad_scores = (probabilities * (grad_probs - delta[:, :, None])).astype(jnp.bfloat16)
        return (probabilities.astype(jnp.bfloat16), grad_scores)

    def backward_tile(carried, query, keys, values, key_index, log_total, delta):
        grad_query, grad_key, grad_value = carried
        weights, grad_scores = tile_grads(
            query, upstream_heads, keys, values, own_index, key_index, log_total, delta
        )
        grad_value = grad_value + jnp.einsum(
            "hij,ihd->jhd", weights, upstream_heads, preferred_element_type=jnp.float32
        ).reshape(row_count, feature_count)
        grad_query = grad_query + jnp.einsum(
            "hij,jhd->ihd", grad_scores, split_heads(keys), preferred_element_type=jnp.float32
        )
        grad_key = grad_key + jnp.einsum(
            "hij,ihd->jhd", grad_scores, split_heads(query), preferred_element_type=jnp.float32
        ).reshape(row_count, feature_count)
        return (grad_query, grad_key, grad_value)

    def backward_apply(carried, query, keys, values, key_index, log_total, delta):
        return backward_tile(carried, query, keys, values, key_index, log_total, delta)

    def pass_blocks(blocks):
        key_a, value_a, key_b, value_b, index_block = blocks
        return passed_along((key_a, value_a, key_b, value_b, index_block), "ctx", 1)

    start = (key_own, value_own, partner_key, partner_value, block_slot)
    initial = (
        jnp.full((HEADS, row_count), -1e30, jnp.float32),
        jnp.zeros((HEADS, row_count), jnp.float32),
        jnp.zeros((row_count, HEADS, HEAD), jnp.float32),
    )
    state_self = forward_apply(initial, query_s, key_own, value_own, own_index)
    state_cross = forward_apply(initial, query_c, partner_key, partner_value, own_index)

    def forward_step(carry, unused):
        blocks, carried_self, carried_cross = carry
        blocks = pass_blocks(blocks)
        key_index = blocks[4][0]
        carried_self = forward_apply(carried_self, query_s, blocks[0], blocks[1], key_index)
        carried_cross = forward_apply(carried_cross, query_c, blocks[2], blocks[3], key_index)
        return ((blocks, carried_self, carried_cross), None)

    (unused_end, state_self, state_cross), stored = lax.scan(
        forward_step, (start, state_self, state_cross), None, length=group_size - 1
    )

    def finish(carried):
        row_max, row_total, accumulated = carried
        return (accumulated / row_total.T[:, :, None], row_max + jnp.log(row_total))

    output_self, log_self = finish(state_self)
    output_cross, log_cross = finish(state_cross)
    layer_out = (output_self + output_cross).reshape(row_count, feature_count).astype(jnp.bfloat16)
    upstream_wide = upstream_heads.astype(jnp.float32)
    delta_self = jnp.sum(upstream_wide * output_self, axis=2).T
    delta_cross = jnp.sum(upstream_wide * output_cross, axis=2).T
    zero_rows = jnp.zeros((row_count, feature_count), jnp.float32)
    zero_query = jnp.zeros((row_count, HEADS, HEAD), jnp.float32)

    def pass_grads(gradients):
        first, second, third, fourth = gradients
        return (
            passed_along(first.astype(jnp.bfloat16), "ctx", 1).astype(first.dtype),
            passed_along(second.astype(jnp.bfloat16), "ctx", 1).astype(second.dtype),
            passed_along(third.astype(jnp.bfloat16), "ctx", 1).astype(third.dtype),
            passed_along(fourth.astype(jnp.bfloat16), "ctx", 1).astype(fourth.dtype),
        )

    qgrad_self, kgrad_self, vgrad_self = backward_apply(
        (zero_query, zero_rows, zero_rows),
        query_s,
        key_own,
        value_own,
        own_index,
        log_self,
        delta_self,
    )
    qgrad_cross, kgrad_cross, vgrad_cross = backward_apply(
        (zero_query, zero_rows, zero_rows),
        query_c,
        partner_key,
        partner_value,
        own_index,
        log_cross,
        delta_cross,
    )

    def backward_step(carry, stored_blocks):
        blocks, gradients, query_grad_s, query_grad_c = carry
        gradients = pass_grads(gradients)
        blocks = pass_blocks(blocks)
        key_index = blocks[4][0]
        query_grad_s, key_grad_s, value_grad_s = backward_apply(
            (query_grad_s, gradients[0], gradients[1]),
            query_s,
            blocks[0],
            blocks[1],
            key_index,
            log_self,
            delta_self,
        )
        query_grad_c, key_grad_c, value_grad_c = backward_apply(
            (query_grad_c, gradients[2], gradients[3]),
            query_c,
            blocks[2],
            blocks[3],
            key_index,
            log_cross,
            delta_cross,
        )
        return (
            (
                blocks,
                (key_grad_s, value_grad_s, key_grad_c, value_grad_c),
                query_grad_s,
                query_grad_c,
            ),
            None,
        )

    (unused_end, gradients, qgrad_self, qgrad_cross), unused_ys = lax.scan(
        backward_step,
        (start, (kgrad_self, vgrad_self, kgrad_cross, vgrad_cross), qgrad_self, qgrad_cross),
        stored,
        length=group_size - 1,
    )
    gradients = (
        passed_along(gradients[0].astype(jnp.bfloat16), "ctx", -(group_size - 1)).astype(
            jnp.float32
        ),
        passed_along(gradients[1].astype(jnp.bfloat16), "ctx", -(group_size - 1)).astype(
            jnp.float32
        ),
        passed_along(gradients[2].astype(jnp.bfloat16), "ctx", -(group_size - 1)).astype(
            jnp.float32
        ),
        passed_along(gradients[3].astype(jnp.bfloat16), "ctx", -(group_size - 1)).astype(
            jnp.float32
        ),
    )
    key_home_self, value_home_self = (gradients[0], gradients[1])
    home_key, home_value = swapped((as_sent(gradients[2]), as_sent(gradients[3])), "tower", 0)
    return (
        layer_out[None],
        (qgrad_self * score_scale).reshape(row_count, feature_count).astype(jnp.bfloat16)[None],
        (key_home_self * score_scale).astype(jnp.bfloat16)[None],
        value_home_self.astype(jnp.bfloat16)[None],
        (qgrad_cross * score_scale).reshape(row_count, feature_count).astype(jnp.bfloat16)[None],
        (home_key * score_scale).astype(jnp.bfloat16)[None],
        home_value.astype(jnp.bfloat16)[None],
    )


def solution(mesh):
    return jax.shard_map(
        body,
        mesh=mesh,
        in_specs=(
            P("tower", ("dp", "ctx"), None),
            P("tower", ("dp", "ctx"), None),
            P("tower", ("dp", "ctx"), None),
            P("tower", ("dp", "ctx"), None),
            P("tower", ("dp", "ctx"), None),
            P("tower", ("dp", "ctx"), None),
            P("tower", ("dp", "ctx"), None),
            P("ctx"),
        ),
        out_specs=(
            P("tower", ("dp", "ctx"), None),
            P("tower", ("dp", "ctx"), None),
            P("tower", ("dp", "ctx"), None),
            P("tower", ("dp", "ctx"), None),
            P("tower", ("dp", "ctx"), None),
            P("tower", ("dp", "ctx"), None),
            P("tower", ("dp", "ctx"), None),
        ),
        check_vma=False,
    )
```

profile of v0, /device:TPU:38, one launch (start us, length us, event | category | flops | bytes accessed | tf_op | source)
XLA Modules:
  0.0 646.9 jit_solution(1400368097622248013)
XLA Ops:
  1.7 15.0 %collective-permute-start.14 = (bf16[128,512]{0,1:T(8,128)(2,1)S(1)}, bf16[128,512]{0,1:T(8,128)(2,1)S(1)}, u32[]{:S(2)}, u32[]{:S(2)}) collective-permute-start(bf16[128,512]{0,1:T(8,128)(2,1)S(1)} %bitcast.296), channel_id=1, source_target_pairs={{0,256},{256,0},{1,257},{257,1},{2,258},{258,2},{3,259},{259,3},{4... | collective-permute-start | bytes 393224 | tf_op jit(solution)/shard_map/ppermute | solution.py:13
  24.0 5.9 collective-permute-done.14
  30.4 9.5 %collective-permute-done.15 = bf16[128,512]{0,1:T(8,128)(2,1)S(1)} collective-permute-done((bf16[128,512]{0,1:T(8,128)(2,1)S(1)}, bf16[128,512]{0,1:T(8,128)(2,1)S(1)}, u32[]{:S(2)}, u32[]{:S(2)}) %collective-permute-start.15) | collective-permute-done | bytes 131104 | tf_op jit(solution)/shard_map/ppermute | solution.py:13
  40.8 180.8 %while.68 = (s32[]{:T(128)}, bf16[128,512]{0,1:T(8,128)(2,1)S(1)}, bf16[128,512]{0,1:T(8,128)(2,1)S(1)}, bf16[128,512]{0,1:T(8,128)(2,1)S(1)}, bf16[128,512]{0,1...) while((s32[]{:T(128)}, bf16[128,512]{0,1:T(8,128)(2,1)S(1)}, ...), condition=%wide.region_9.10_spmd.clone.clone, body=%wide.region_4.9_spmd.clone.clone.sunk | while | flops 69228800 | bytes 8309137 | solution.py:130
  118.5 7.2 %collective-permute-start.3 = (bf16[128,512]{0,1:T(8,128)(2,1)}, bf16[128,512]{0,1:T(8,128)(2,1)S(1)}, u32[]{:S(2)}, u32[]{:S(2)}) collective-permute-start(bf16[128,512]{0,1:T(8,128)(2,1)} %get-tuple-element.1027), channel_id=1, source_target_pairs={{254,0},{0,2},{2,4},{4,6},{6,8},{8,10},{10,12},{12,14},{14,16},{16... | collective-permute-start | bytes 393224 | tf_op jit(solution)/shard_map/while/body/eval_jaxpr/ppermute | solution.py:19
  142.3 6.5 collective-permute-start
  148.8 8.6 %collective-permute-start.3 = (bf16[128,512]{0,1:T(8,128)(2,1)}, bf16[128,512]{0,1:T(8,128)(2,1)S(1)}, u32[]{:S(2)}, u32[]{:S(2)}) collective-permute-start(bf16[128,512]{0,1:T(8,128)(2,1)} %get-tuple-element.1027), channel_id=1, source_target_pairs={{254,0},{0,2},{2,4},{4,6},{6,8},{8,10},{10,12},{12,14},{14,16},{16... | collective-permute-start | bytes 393224 | tf_op jit(solution)/shard_map/while/body/eval_jaxpr/ppermute | solution.py:19
  161.2 6.5 %collective-permute-done.1 = bf16[128,512]{0,1:T(8,128)(2,1)S(1)} collective-permute-done((bf16[128,512]{0,1:T(8,128)(2,1)S(1)}, bf16[128,512]{0,1:T(8,128)(2,1)S(1)}, u32[]{:S(2)}, u32[]{:S(2)}) %collective-permute-start.1) | collective-permute-done | bytes 131104 | tf_op jit(solution)/shard_map/while/body/eval_jaxpr/ppermute | solution.py:19
  176.3 8.4 %collective-permute-start.3 = (bf16[128,512]{0,1:T(8,128)(2,1)}, bf16[128,512]{0,1:T(8,128)(2,1)S(1)}, u32[]{:S(2)}, u32[]{:S(2)}) collective-permute-start(bf16[128,512]{0,1:T(8,128)(2,1)} %get-tuple-element.1027), channel_id=1, source_target_pairs={{254,0},{0,2},{2,4},{4,6},{6,8},{8,10},{10,12},{12,14},{14,16},{16... | collective-permute-start | bytes 393224 | tf_op jit(solution)/shard_map/while/body/eval_jaxpr/ppermute | solution.py:19
  202.3 7.3 %collective-permute-start.3 = (bf16[128,512]{0,1:T(8,128)(2,1)}, bf16[128,512]{0,1:T(8,128)(2,1)S(1)}, u32[]{:S(2)}, u32[]{:S(2)}) collective-permute-start(bf16[128,512]{0,1:T(8,128)(2,1)} %get-tuple-element.1027), channel_id=1, source_target_pairs={{254,0},{0,2},{2,4},{4,6},{6,8},{8,10},{10,12},{12,14},{14,16},{16... | collective-permute-start | bytes 393224 | tf_op jit(solution)/shard_map/while/body/eval_jaxpr/ppermute | solution.py:19
  213.4 6.5 %collective-permute-done.1 = bf16[128,512]{0,1:T(8,128)(2,1)S(1)} collective-permute-done((bf16[128,512]{0,1:T(8,128)(2,1)S(1)}, bf16[128,512]{0,1:T(8,128)(2,1)S(1)}, u32[]{:S(2)}, u32[]{:S(2)}) %collective-permute-start.1) | collective-permute-done | bytes 131104 | tf_op jit(solution)/shard_map/while/body/eval_jaxpr/ppermute | solution.py:19
  223.8 279.4 %while.69 = (s32[]{:T(128)}, bf16[128,512]{0,1:T(8,128)(2,1)S(1)}, bf16[128,512]{0,1:T(8,128)(2,1)S(1)}, bf16[128,512]{0,1:T(8,128)(2,1)S(1)}, bf16[128,512]{0,1...) while((s32[]{:T(128)}, bf16[128,512]{0,1:T(8,128)(2,1)S(1)}, ...), condition=%wide.region_13.14_spmd.clone.clone, body=%wide.region_12.13_spmd.clone.clone.sunk | while | flops 170541312 | bytes 16058969 | solution.py:208
  230.9 5.8 collective-permute-start.12
  270.1 8.6 %collective-permute-start.12 = (bf16[128,512]{0,1:T(8,128)(2,1)S(1)}, bf16[128,512]{0,1:T(8,128)(2,1)S(1)}, u32[]{:S(2)}, u32[]{:S(2)}) collective-permute-start(bf16[128,512]{0,1:T(8,128)(2,1)S(1)} %get-tuple-element.1087), channel_id=1, source_target_pairs={{254,0},{0,2},{2,4},{4,6},{6,8},{8,10},{10,12},{12,14},{14,16},{16... | collective-permute-start | bytes 393224 | tf_op jit(solution)/shard_map/while/body/eval_jaxpr/ppermute | solution.py:19
  308.8 6.4 collective-permute-start.12
  345.4 7.9 %collective-permute-start.12 = (bf16[128,512]{0,1:T(8,128)(2,1)S(1)}, bf16[128,512]{0,1:T(8,128)(2,1)S(1)}, u32[]{:S(2)}, u32[]{:S(2)}) collective-permute-start(bf16[128,512]{0,1:T(8,128)(2,1)S(1)} %get-tuple-element.1087), channel_id=1, source_target_pairs={{254,0},{0,2},{2,4},{4,6},{6,8},{8,10},{10,12},{12,14},{14,16},{16... | collective-permute-start | bytes 393224 | tf_op jit(solution)/shard_map/while/body/eval_jaxpr/ppermute | solution.py:19
  385.1 8.6 %collective-permute-start.12 = (bf16[128,512]{0,1:T(8,128)(2,1)S(1)}, bf16[128,512]{0,1:T(8,128)(2,1)S(1)}, u32[]{:S(2)}, u32[]{:S(2)}) collective-permute-start(bf16[128,512]{0,1:T(8,128)(2,1)S(1)} %get-tuple-element.1087), channel_id=1, source_target_pairs={{254,0},{0,2},{2,4},{4,6},{6,8},{8,10},{10,12},{12,14},{14,16},{16... | collective-permute-start | bytes 393224 | tf_op jit(solution)/shard_map/while/body/eval_jaxpr/ppermute | solution.py:19
  426.7 6.5 collective-permute-start.8
  433.2 8.6 %collective-permute-start.12 = (bf16[128,512]{0,1:T(8,128)(2,1)S(1)}, bf16[128,512]{0,1:T(8,128)(2,1)S(1)}, u32[]{:S(2)}, u32[]{:S(2)}) collective-permute-start(bf16[128,512]{0,1:T(8,128)(2,1)S(1)} %get-tuple-element.1087), channel_id=1, source_target_pairs={{254,0},{0,2},{2,4},{4,6},{6,8},{8,10},{10,12},{12,14},{14,16},{16... | collective-permute-start | bytes 393224 | tf_op jit(solution)/shard_map/while/body/eval_jaxpr/ppermute | solution.py:19
  473.5 8.2 %collective-permute-start.12 = (bf16[128,512]{0,1:T(8,128)(2,1)S(1)}, bf16[128,512]{0,1:T(8,128)(2,1)S(1)}, u32[]{:S(2)}, u32[]{:S(2)}) collective-permute-start(bf16[128,512]{0,1:T(8,128)(2,1)S(1)} %get-tuple-element.1087), channel_id=1, source_target_pairs={{254,0},{0,2},{2,4},{4,6},{6,8},{8,10},{10,12},{12,14},{14,16},{16... | collective-permute-start | bytes 393224 | tf_op jit(solution)/shard_map/while/body/eval_jaxpr/ppermute | solution.py:19
  509.1 15.3 %collective-permute-start.17 = (bf16[128,512]{1,0:T(8,128)(2,1)S(1)}, bf16[128,512]{1,0:T(8,128)(2,1)S(1)}, u32[]{:S(2)}, u32[]{:S(2)}) collective-permute-start(bf16[128,512]{1,0:T(8,128)(2,1)S(1)} %copy.77), channel_id=1, source_target_pairs={{14,0},{16,2},{18,4},{20,6},{22,8},{24,10},{26,12},{28,14},{30,16}... | collective-permute-start | bytes 393224 | tf_op jit(solution)/shard_map/ppermute | solution.py:19
  524.5 92.5 %collective-permute-start.16 = (bf16[128,512]{1,0:T(8,128)(2,1)S(1)}, bf16[128,512]{1,0:T(8,128)(2,1)S(1)}, u32[]{:S(2)}, u32[]{:S(2)}) collective-permute-start(bf16[128,512]{1,0:T(8,128)(2,1)S(1)} %copy.76), channel_id=1, source_target_pairs={{14,0},{16,2},{18,4},{20,6},{22,8},{24,10},{26,12},{28,14},{30,16}... | collective-permute-start | bytes 393224 | tf_op jit(solution)/shard_map/ppermute | solution.py:19
  619.3 10.0 %collective-permute-start.21 = (bf16[128,512]{1,0:T(8,128)(2,1)S(1)}, bf16[128,512]{1,0:T(8,128)(2,1)S(1)}, u32[]{:S(2)}, u32[]{:S(2)}) collective-permute-start(bf16[128,512]{1,0:T(8,128)(2,1)S(1)} %collective-permute-done.20), channel_id=1, source_target_pairs={{0,256},{256,0},{1,257},{257,1},{2,258},{258,2},{3,259},{259,3},{4... | collective-permute-start | bytes 393224 | tf_op jit(solution)/shard_map/ppermute | solution.py:13
  635.9 9.0 %collective-permute-done.19 = bf16[128,512]{1,0:T(8,128)(2,1)S(1)} collective-permute-done((bf16[128,512]{1,0:T(8,128)(2,1)S(1)}, bf16[128,512]{1,0:T(8,128)(2,1)S(1)}, u32[]{:S(2)}, u32[]{:S(2)}) %collective-permute-start.19) | collective-permute-done | bytes 131104 | tf_op jit(solution)/shard_map/ppermute | solution.py:13
  (528 shorter events, 356.0 us)
Async XLA Ops:
  1.7 28.3 %collective-permute-start.14 = (bf16[128,512]{0,1:T(8,128)(2,1)S(1)}, bf16[128,512]{0,1:T(8,128)(2,1)S(1)}, u32[]{:S(2)}, u32[]{:S(2)}) collective-permute-start(bf16[128,512]{0,1:T(8,128)(2,1)S(1)} %bitcast.296), channel_id=1, source_target_pairs={{0,256},{256,0},{1,257},{257,1},{2,258},{258,2},{3,259},{259,3},{4... | collective-permute-start | bytes 393224 | tf_op jit(solution)/shard_map/ppermute | solution.py:13
  16.8 23.1 %collective-permute-start.15 = (bf16[128,512]{0,1:T(8,128)(2,1)S(1)}, bf16[128,512]{0,1:T(8,128)(2,1)S(1)}, u32[]{:S(2)}, u32[]{:S(2)}) collective-permute-start(bf16[128,512]{0,1:T(8,128)(2,1)S(1)} %bitcast.295), channel_id=1, source_target_pairs={{0,256},{256,0},{1,257},{257,1},{2,258},{258,2},{3,259},{259,3},{4... | collective-permute-start | bytes 393224 | tf_op jit(solution)/shard_map/ppermute | solution.py:13
  136.3 23.0 %collective-permute-start.4 = (s32[1]{0:T(128)}, s32[1]{0:T(128)}, u32[]{:S(2)}, u32[]{:S(2)}) collective-permute-start(s32[1]{0:T(128)} %copy.112), channel_id=1, source_target_pairs={{254,0},{0,2},{2,4},{4,6},{6,8},{8,10},{10,12},{12,14},{14,16},{16... | collective-permute-start | bytes 20 | tf_op jit(solution)/shard_map/while/body/eval_jaxpr/ppermute | solution.py:19
  230.9 21.9 %collective-permute-start.12 = (bf16[128,512]{0,1:T(8,128)(2,1)S(1)}, bf16[128,512]{0,1:T(8,128)(2,1)S(1)}, u32[]{:S(2)}, u32[]{:S(2)}) collective-permute-start(bf16[128,512]{0,1:T(8,128)(2,1)S(1)} %get-tuple-element.1087), channel_id=1, source_target_pairs={{254,0},{0,2},{2,4},{4,6},{6,8},{8,10},{10,12},{12,14},{14,16},{16... | collective-permute-start | bytes 393224 | tf_op jit(solution)/shard_map/while/body/eval_jaxpr/ppermute | solution.py:19
  259.5 21.1 %collective-permute-start.9 = (s32[1]{0:T(128)}, s32[1]{0:T(128)}, u32[]{:S(2)}, u32[]{:S(2)}) collective-permute-start(s32[1]{0:T(128)} %copy.148), channel_id=1, source_target_pairs={{254,0},{0,2},{2,4},{4,6},{6,8},{8,10},{10,12},{12,14},{14,16},{16... | collective-permute-start | bytes 20 | tf_op jit(solution)/shard_map/while/body/eval_jaxpr/ppermute | solution.py:19
  265.6 24.5 %collective-permute-start.8 = (bf16[128,512]{0,1:T(8,128)(2,1)S(1)}, bf16[128,512]{0,1:T(8,128)(2,1)S(1)}, u32[]{:S(2)}, u32[]{:S(2)}) collective-permute-start(bf16[128,512]{0,1:T(8,128)(2,1)S(1)} %get-tuple-element.1083), channel_id=1, source_target_pairs={{254,0},{0,2},{2,4},{4,6},{6,8},{8,10},{10,12},{12,14},{14,16},{16... | collective-permute-start | bytes 393224 | tf_op jit(solution)/shard_map/while/body/eval_jaxpr/ppermute | solution.py:19
  270.1 23.7 %collective-permute-start.12 = (bf16[128,512]{0,1:T(8,128)(2,1)S(1)}, bf16[128,512]{0,1:T(8,128)(2,1)S(1)}, u32[]{:S(2)}, u32[]{:S(2)}) collective-permute-start(bf16[128,512]{0,1:T(8,128)(2,1)S(1)} %get-tuple-element.1087), channel_id=1, source_target_pairs={{254,0},{0,2},{2,4},{4,6},{6,8},{8,10},{10,12},{12,14},{14,16},{16... | collective-permute-start | bytes 393224 | tf_op jit(solution)/shard_map/while/body/eval_jaxpr/ppermute | solution.py:19
  304.9 21.7 %collective-permute-start.8 = (bf16[128,512]{0,1:T(8,128)(2,1)S(1)}, bf16[128,512]{0,1:T(8,128)(2,1)S(1)}, u32[]{:S(2)}, u32[]{:S(2)}) collective-permute-start(bf16[128,512]{0,1:T(8,128)(2,1)S(1)} %get-tuple-element.1083), channel_id=1, source_target_pairs={{254,0},{0,2},{2,4},{4,6},{6,8},{8,10},{10,12},{12,14},{14,16},{16... | collective-permute-start | bytes 393224 | tf_op jit(solution)/shard_map/while/body/eval_jaxpr/ppermute | solution.py:19
  308.8 21.6 %collective-permute-start.12 = (bf16[128,512]{0,1:T(8,128)(2,1)S(1)}, bf16[128,512]{0,1:T(8,128)(2,1)S(1)}, u32[]{:S(2)}, u32[]{:S(2)}) collective-permute-start(bf16[128,512]{0,1:T(8,128)(2,1)S(1)} %get-tuple-element.1087), channel_id=1, source_target_pairs={{254,0},{0,2},{2,4},{4,6},{6,8},{8,10},{10,12},{12,14},{14,16},{16... | collective-permute-start | bytes 393224 | tf_op jit(solution)/shard_map/while/body/eval_jaxpr/ppermute | solution.py:19
  341.8 23.0 %collective-permute-start.8 = (bf16[128,512]{0,1:T(8,128)(2,1)S(1)}, bf16[128,512]{0,1:T(8,128)(2,1)S(1)}, u32[]{:S(2)}, u32[]{:S(2)}) collective-permute-start(bf16[128,512]{0,1:T(8,128)(2,1)S(1)} %get-tuple-element.1083), channel_id=1, source_target_pairs={{254,0},{0,2},{2,4},{4,6},{6,8},{8,10},{10,12},{12,14},{14,16},{16... | collective-permute-start | bytes 393224 | tf_op jit(solution)/shard_map/while/body/eval_jaxpr/ppermute | solution.py:19
  345.4 23.1 %collective-permute-start.12 = (bf16[128,512]{0,1:T(8,128)(2,1)S(1)}, bf16[128,512]{0,1:T(8,128)(2,1)S(1)}, u32[]{:S(2)}, u32[]{:S(2)}) collective-permute-start(bf16[128,512]{0,1:T(8,128)(2,1)S(1)} %get-tuple-element.1087), channel_id=1, source_target_pairs={{254,0},{0,2},{2,4},{4,6},{6,8},{8,10},{10,12},{12,14},{14,16},{16... | collective-permute-start | bytes 393224 | tf_op jit(solution)/shard_map/while/body/eval_jaxpr/ppermute | solution.py:19
  374.4 21.3 %collective-permute-start.9 = (s32[1]{0:T(128)}, s32[1]{0:T(128)}, u32[]{:S(2)}, u32[]{:S(2)}) collective-permute-start(s32[1]{0:T(128)} %copy.148), channel_id=1, source_target_pairs={{254,0},{0,2},{2,4},{4,6},{6,8},{8,10},{10,12},{12,14},{14,16},{16... | collective-permute-start | bytes 20 | tf_op jit(solution)/shard_map/while/body/eval_jaxpr/ppermute | solution.py:19
  379.5 27.9 %collective-permute-start.8 = (bf16[128,512]{0,1:T(8,128)(2,1)S(1)}, bf16[128,512]{0,1:T(8,128)(2,1)S(1)}, u32[]{:S(2)}, u32[]{:S(2)}) collective-permute-start(bf16[128,512]{0,1:T(8,128)(2,1)S(1)} %get-tuple-element.1083), channel_id=1, source_target_pairs={{254,0},{0,2},{2,4},{4,6},{6,8},{8,10},{10,12},{12,14},{14,16},{16... | collective-permute-start | bytes 393224 | tf_op jit(solution)/shard_map/while/body/eval_jaxpr/ppermute | solution.py:19
  385.1 26.0 %collective-permute-start.12 = (bf16[128,512]{0,1:T(8,128)(2,1)S(1)}, bf16[128,512]{0,1:T(8,128)(2,1)S(1)}, u32[]{:S(2)}, u32[]{:S(2)}) collective-permute-start(bf16[128,512]{0,1:T(8,128)(2,1)S(1)} %get-tuple-element.1087), channel_id=1, source_target_pairs={{254,0},{0,2},{2,4},{4,6},{6,8},{8,10},{10,12},{12,14},{14,16},{16... | collective-permute-start | bytes 393224 | tf_op jit(solution)/shard_map/while/body/eval_jaxpr/ppermute | solution.py:19
  418.0 25.7 %collective-permute-start.9 = (s32[1]{0:T(128)}, s32[1]{0:T(128)}, u32[]{:S(2)}, u32[]{:S(2)}) collective-permute-start(s32[1]{0:T(128)} %copy.148), channel_id=1, source_target_pairs={{254,0},{0,2},{2,4},{4,6},{6,8},{8,10},{10,12},{12,14},{14,16},{16... | collective-permute-start | bytes 20 | tf_op jit(solution)/shard_map/while/body/eval_jaxpr/ppermute | solution.py:19
  421.2 25.2 %collective-permute-start.7 = (bf16[128,512]{0,1:T(8,128)(2,1)S(1)}, bf16[128,512]{0,1:T(8,128)(2,1)S(1)}, u32[]{:S(2)}, u32[]{:S(2)}) collective-permute-start(bf16[128,512]{0,1:T(8,128)(2,1)S(1)} %get-tuple-element.1082), channel_id=1, source_target_pairs={{254,0},{0,2},{2,4},{4,6},{6,8},{8,10},{10,12},{12,14},{14,16},{16... | collective-permute-start | bytes 393224 | tf_op jit(solution)/shard_map/while/body/eval_jaxpr/ppermute | solution.py:19
  426.7 27.6 %collective-permute-start.8 = (bf16[128,512]{0,1:T(8,128)(2,1)S(1)}, bf16[128,512]{0,1:T(8,128)(2,1)S(1)}, u32[]{:S(2)}, u32[]{:S(2)}) collective-permute-start(bf16[128,512]{0,1:T(8,128)(2,1)S(1)} %get-tuple-element.1083), channel_id=1, source_target_pairs={{254,0},{0,2},{2,4},{4,6},{6,8},{8,10},{10,12},{12,14},{14,16},{16... | collective-permute-start | bytes 393224 | tf_op jit(solution)/shard_map/while/body/eval_jaxpr/ppermute | solution.py:19
  433.2 24.8 %collective-permute-start.12 = (bf16[128,512]{0,1:T(8,128)(2,1)S(1)}, bf16[128,512]{0,1:T(8,128)(2,1)S(1)}, u32[]{:S(2)}, u32[]{:S(2)}) collective-permute-start(bf16[128,512]{0,1:T(8,128)(2,1)S(1)} %get-tuple-element.1087), channel_id=1, source_target_pairs={{254,0},{0,2},{2,4},{4,6},{6,8},{8,10},{10,12},{12,14},{14,16},{16... | collective-permute-start | bytes 393224 | tf_op jit(solution)/shard_map/while/body/eval_jaxpr/ppermute | solution.py:19
  470.5 22.7 %collective-permute-start.8 = (bf16[128,512]{0,1:T(8,128)(2,1)S(1)}, bf16[128,512]{0,1:T(8,128)(2,1)S(1)}, u32[]{:S(2)}, u32[]{:S(2)}) collective-permute-start(bf16[128,512]{0,1:T(8,128)(2,1)S(1)} %get-tuple-element.1083), channel_id=1, source_target_pairs={{254,0},{0,2},{2,4},{4,6},{6,8},{8,10},{10,12},{12,14},{14,16},{16... | collective-permute-start | bytes 393224 | tf_op jit(solution)/shard_map/while/body/eval_jaxpr/ppermute | solution.py:19
  473.5 23.4 %collective-permute-start.12 = (bf16[128,512]{0,1:T(8,128)(2,1)S(1)}, bf16[128,512]{0,1:T(8,128)(2,1)S(1)}, u32[]{:S(2)}, u32[]{:S(2)}) collective-permute-start(bf16[128,512]{0,1:T(8,128)(2,1)S(1)} %get-tuple-element.1087), channel_id=1, source_target_pairs={{254,0},{0,2},{2,4},{4,6},{6,8},{8,10},{10,12},{12,14},{14,16},{16... | collective-permute-start | bytes 393224 | tf_op jit(solution)/shard_map/while/body/eval_jaxpr/ppermute | solution.py:19
  503.4 116.0 %collective-permute-start.20 = (bf16[128,512]{1,0:T(8,128)(2,1)S(1)}, bf16[128,512]{1,0:T(8,128)(2,1)S(1)}, u32[]{:S(2)}, u32[]{:S(2)}) collective-permute-start(bf16[128,512]{1,0:T(8,128)(2,1)S(1)} %copy.79), channel_id=1, source_target_pairs={{14,0},{16,2},{18,4},{20,6},{22,8},{24,10},{26,12},{28,14},{30,16}... | collective-permute-start | bytes 393224 | tf_op jit(solution)/shard_map/ppermute | solution.py:19
  505.4 123.9 %collective-permute-start.18 = (bf16[128,512]{1,0:T(8,128)(2,1)S(1)}, bf16[128,512]{1,0:T(8,128)(2,1)S(1)}, u32[]{:S(2)}, u32[]{:S(2)}) collective-permute-start(bf16[128,512]{1,0:T(8,128)(2,1)S(1)} %copy.78), channel_id=1, source_target_pairs={{14,0},{16,2},{18,4},{20,6},{22,8},{24,10},{26,12},{28,14},{30,16}... | collective-permute-start | bytes 393224 | tf_op jit(solution)/shard_map/ppermute | solution.py:19
  509.1 110.3 %collective-permute-start.17 = (bf16[128,512]{1,0:T(8,128)(2,1)S(1)}, bf16[128,512]{1,0:T(8,128)(2,1)S(1)}, u32[]{:S(2)}, u32[]{:S(2)}) collective-permute-start(bf16[128,512]{1,0:T(8,128)(2,1)S(1)} %copy.77), channel_id=1, source_target_pairs={{14,0},{16,2},{18,4},{20,6},{22,8},{24,10},{26,12},{28,14},{30,16}... | collective-permute-start | bytes 393224 | tf_op jit(solution)/shard_map/ppermute | solution.py:19
  524.5 109.4 %collective-permute-start.16 = (bf16[128,512]{1,0:T(8,128)(2,1)S(1)}, bf16[128,512]{1,0:T(8,128)(2,1)S(1)}, u32[]{:S(2)}, u32[]{:S(2)}) collective-permute-start(bf16[128,512]{1,0:T(8,128)(2,1)S(1)} %copy.76), channel_id=1, source_target_pairs={{14,0},{16,2},{18,4},{20,6},{22,8},{24,10},{26,12},{28,14},{30,16}... | collective-permute-start | bytes 393224 | tf_op jit(solution)/shard_map/ppermute | solution.py:19
  (88 other events, 1056.4 us)
where the time goes:
time: 650 us; the launch traced here: 647 us
  starting transfers between devices  455 us (70%)
  waiting for transfers between devices  120 us (18%)
  matrix products  29.5 us (5%)
  loops' own time  20.6 us (3%)
  local copies, waits for them, and re-layouts  14.9 us (2%)
    ppermute x102, starting transfers between devices, passed_along(): return lax.ppermute(block, axis, route)  423 us
    ppermute x102, waiting for transfers between devices, passed_along(): return lax.ppermute(block, axis, route)  94.2 us
    ppermute x4, starting transfers between devices, swapped(): return lax.ppermute(value, axis, pairs)  31.4 us
    ppermute x4, waiting for transfers between devices, swapped(): return lax.ppermute(value, axis, pairs)  25.7 us
  transfers between devices with their start and end apart: 106, of which 36 were waited for; matrix products, arithmetic and copies ran while one was open for 5% of the time, Pallas kernels for 0%

commit v1 on v0

v1 whole, which is shorter than its diff:
```python
import jax
import jax.numpy as jnp
from jax import lax
from jax.experimental import pallas as pl
from jax.experimental.pallas import tpu as pltpu
from jax.sharding import PartitionSpec as P

HEADS = 8
HEAD = 64
ROWS = 128
GROUP = 8
TEAM = 8
PAIR = 2 * HEAD
BOTH = 2 * ROWS
HALO = GROUP - 1
WINDOW = GROUP * ROWS
SPAN = (HALO + TEAM) * ROWS
FEATURES = HEADS * HEAD
VMEM_BYTES = 48 * 1024 * 1024
SELF, CROSS, NEAR, FAR = 0, 1, 2, 3


def vmem(count):
    return [pl.BlockSpec(memory_space=pltpu.VMEM)] * count


def smem():
    return [pl.BlockSpec(memory_space=pltpu.SMEM)]


def block_shape(*lead, dtype=jnp.bfloat16):
    return jax.ShapeDtypeStruct((*lead, ROWS, PAIR), dtype)


def paired(left, right, h):
    lanes = pl.ds(h * HEAD, HEAD)
    return jnp.concatenate([left[:, lanes], right[:, lanes]], axis=1)


def my_flip():
    return lax.rem(lax.axis_index("ctx") // TEAM, 2) * (TEAM // 2)


def pack_kernel(
    query_s, key_s, value_s, query_c, key_c, value_c, upstream, out, held, arrived
):
    sources = (upstream, query_c, query_s, key_s, value_s, key_c, value_c)
    copies = [
        pltpu.make_async_copy(source, held.at[i], arrived.at[i])
        for i, source in enumerate(sources)
    ]
    for copy in copies:
        copy.start()
    flip = my_flip()
    copies[0].wait()
    for kind, left, right in ((FAR, 1, 0), (NEAR, 2, 0), (SELF, 3, 4), (CROSS, 5, 6)):
        copies[left].wait()
        if right:
            copies[right].wait()
        for h in range(HEADS):
            out[jnp.bitwise_xor(h, flip), kind] = paired(held.at[left], held.at[right], h)


def attention_kernel(kind, slots, *refs):
    if kind == SELF:
        own, halo, out, dkv_own, dkv_halo, kv_t, scores, probs, stacks = refs
        queries = [own.at[b, NEAR] for b in range(TEAM)]
    else:
        qdo, own, halo, out, dkv_own, dkv_halo, kv_t, scores, probs, stacks = refs
        queries = [qdo.at[b] for b in range(TEAM)]
    blocks = [halo.at[b, kind] for b in range(HALO)] + [own.at[b, kind] for b in range(TEAM)]
    first_half = lax.broadcasted_iota(jnp.int32, (ROWS, PAIR), 1) < HEAD
    causal = lax.broadcasted_iota(jnp.int32, (ROWS, ROWS), 0) <= lax.broadcasted_iota(
        jnp.int32, (ROWS, ROWS), 1
    )
    peaks, hidden, sums = {}, {}, {}

    def turn(w):
        kv_t[:, w * ROWS : (w + 1) * ROWS] = blocks[w][...].T

    def begin(m):
        both = queries[m][...]
        none = jnp.zeros_like(both)
        stacks[m * BOTH : m * BOTH + ROWS, :] = jnp.where(
            first_half, both * jnp.bfloat16(HEAD ** (-0.5)), none
        )
        stacks[m * BOTH + ROWS : (m + 1) * BOTH, :] = jnp.where(first_half, none, both)
        slot = lax.rem(slots[0] + m, slots[1])
        hidden[m] = [jnp.where(slot >= HALO - k, 0.0, 1e30) for k in range(HALO)] + [0.0]

    def score(m, k):
        part = lax.dot_general(
            blocks[m + k][...],
            stacks[m * BOTH : (m + 1) * BOTH, :],
            (((1,), (1,)), ((), ())),
            preferred_element_type=jnp.float32,
        )
        logits = part[:, :ROWS]
        if k == GROUP - 1:
            logits = jnp.where(causal, logits, -1e30)
        scores[m % 2, k, :, :ROWS] = logits
        scores[m % 2, k, :, ROWS:] = part[:, ROWS:]
        peak = jnp.max(logits.reshape(ROWS // 8, 8, ROWS), axis=0) - hidden[m][k]
        peaks[m] = peak if k == 0 else jnp.maximum(peaks[m], peak)

    def raise_up(m, k, top):
        raised = jnp.exp(scores[m % 2, k, :, :ROWS] - (top + hidden[m][k]))
        change = raised * scores[m % 2, k, :, ROWS:]
        scores[m % 2, k, :, :ROWS] = raised
        total = jnp.sum(raised.reshape(ROWS // 8, 8, ROWS), axis=0)
        weighted = jnp.sum(change.reshape(ROWS // 8, 8, ROWS), axis=0)
        sums[m] = (total, weighted) if k == 0 else (sums[m][0] + total, sums[m][1] + weighted)

    def settle(m, k, scale, delta):
        weight = scores[m % 2, k, :, :ROWS] * scale
        change = weight * (scores[m % 2, k, :, ROWS:] - delta)
        rows, lanes = slice((m + k) * ROWS, (m + k + 1) * ROWS), m * BOTH
        probs[rows, lanes : lanes + ROWS] = change.astype(jnp.bfloat16)
        probs[rows, lanes + ROWS : lanes + BOTH] = weight.astype(jnp.bfloat16)

    def query_side(m):
        window, lanes = slice(m * ROWS, m * ROWS + WINDOW), m * BOTH
        mixed = lax.dot_general(
            kv_t[:, window],
            probs[window, lanes : lanes + BOTH],
            (((1,), (0,)), ((), ())),
            preferred_element_type=jnp.float32,
        )
        result = jnp.concatenate(
            [mixed[:HEAD, :ROWS] * HEAD ** (-0.5), mixed[HEAD:, ROWS:]], axis=0
        )
        out[m] = result.T.astype(jnp.bfloat16)

    def key_side(w):
        low, high = max(0, w - HALO), min(TEAM - 1, w) + 1
        total = lax.dot_general(
            probs[w * ROWS : (w + 1) * ROWS, low * BOTH : high * BOTH],
            stacks[low * BOTH : high * BOTH, :],
            (((1,), (0,)), ((), ())),
            preferred_element_type=jnp.float32,
        )
        if w < HALO:
            dkv_halo[w] = total.astype(jnp.bfloat16)
        else:
            dkv_own[w - HALO] = total

    begin(0)
    for k in range(GROUP):
        score(0, k)
        turn(k)
    for m in range(TEAM):
        top = jnp.max(peaks[m], axis=0, keepdims=True)
        if m + 1 < TEAM:
            begin(m + 1)
        for k in range(GROUP):
            raise_up(m, k, top)
            if m + 1 < TEAM:
                score(m + 1, k)
        if m + 1 < TEAM:
            turn(m + GROUP)
        scale = 1.0 / jnp.sum(sums[m][0], axis=0, keepdims=True)
        delta = jnp.sum(sums[m][1], axis=0, keepdims=True) * scale
        for k in range(GROUP):
            settle(m, k, scale, delta)
            if m and k == 1:
                query_side(m - 1)
            if m and k == 4:
                key_side(m - 1)
    query_side(TEAM - 1)
    for w in range(TEAM - 1, HALO + TEAM):
        key_side(w)


def attention(kind, *operands):
    def kernel(*refs):
        attention_kernel(kind, *refs)

    return pl.pallas_call(
        kernel,
        out_shape=(
            block_shape(TEAM),
            block_shape(TEAM, dtype=jnp.float32),
            block_shape(HALO),
        ),
        in_specs=smem() + vmem(len(operands) - 1),
        out_specs=tuple(vmem(3)),
        scratch_shapes=[
            pltpu.VMEM((PAIR, SPAN), jnp.bfloat16),
            pltpu.VMEM((2, GROUP, ROWS, BOTH), jnp.float32),
            pltpu.VMEM((SPAN, TEAM * BOTH), jnp.bfloat16),
            pltpu.VMEM((TEAM * BOTH, PAIR), jnp.bfloat16),
        ],
        compiler_params=pltpu.CompilerParams(vmem_limit_bytes=VMEM_BYTES),
        cost_estimate=pl.CostEstimate(flops=0, bytes_accessed=0, transcendentals=0),
        name="attention_cross" if kind == CROSS else "attention_self",
    )(*operands)


def join_kernel(own_s, own_c, home_s, home_c, out_s, out_c, out):
    for kind, own, home in ((SELF, own_s, home_s), (CROSS, own_c, home_c)):
        out[0, kind] = own[0].astype(jnp.bfloat16)
        for b in range(HALO):
            out[b + 1, kind] = (own[b + 1] + home[b].astype(jnp.float32)).astype(jnp.bfloat16)
    for b in range(TEAM):
        out[b, NEAR] = out_s[b]
        out[b, FAR] = out_c[b]


def halves(first, second):
    left = jnp.concatenate([first[:, :HEAD], second[:, :HEAD]], axis=1)
    right = jnp.concatenate([first[:, HEAD:], second[:, HEAD:]], axis=1)
    return left, right


def unpack_kernel(parts, attended, query_s, key_s, value_s, query_c, key_c, value_c):
    flip = my_flip()
    for h in range(0, HEADS, 2):
        lanes = pl.ds(h * HEAD, PAIR)
        first, second = parts.at[jnp.bitwise_xor(h, flip)], parts.at[jnp.bitwise_xor(h + 1, flip)]
        key_s[:, lanes], value_s[:, lanes] = halves(first[SELF], second[SELF])
        key_c[:, lanes], value_c[:, lanes] = halves(first[CROSS], second[CROSS])
        query_s[:, lanes], near = halves(first[NEAR], second[NEAR])
        query_c[:, lanes], far = halves(first[FAR], second[FAR])
        total = near.astype(jnp.float32) + far.astype(jnp.float32)
        attended[:, lanes] = total.astype(jnp.bfloat16)


def local_call(kernel, out_shape, in_specs, operands, name, scratch=()):
    return pl.pallas_call(
        kernel,
        out_shape=out_shape,
        in_specs=in_specs,
        out_specs=jax.tree.map(lambda shape: vmem(1)[0], out_shape),
        scratch_shapes=scratch,
        compiler_params=pltpu.CompilerParams(vmem_limit_bytes=VMEM_BYTES),
        cost_estimate=pl.CostEstimate(flops=0, bytes_accessed=0, transcendentals=0),
        name=name,
    )(*operands)


def to_next_team(value, step):
    count = lax.axis_size("ctx")
    route = [(i, (i + step * TEAM) % count ^ (TEAM // 2)) for i in range(count)]
    return lax.ppermute(value, "ctx", route)


def within_team(value):
    count = lax.axis_size("ctx")
    teams = [list(range(at, at + TEAM)) for at in range(0, count, TEAM)]
    return lax.all_to_all(value, "ctx", 0, 0, axis_index_groups=teams, tiled=True)


def swapped(value):
    return lax.ppermute(value, "tower", [(0, 1), (1, 0)])


def body(
    query_self, key_self, value_self, query_cross, key_cross, value_cross, cotangent, block_slot
):
    count = lax.axis_size("ctx")
    member = lax.rem(lax.axis_index("ctx"), TEAM)
    slots = jnp.stack([lax.rem(block_slot[0] - member + count, count), jnp.int32(count)])
    flat = jax.ShapeDtypeStruct((ROWS, FEATURES), jnp.bfloat16)
    inputs = (query_self, key_self, value_self, query_cross, key_cross, value_cross, cotangent)
    packed = local_call(
        pack_kernel,
        block_shape(TEAM, 4),
        [pl.BlockSpec(memory_space=pltpu.HBM)] * 7,
        tuple(pltpu.with_memory_space_constraint(value[0], pltpu.HBM) for value in inputs),
        "pack",
        [pltpu.VMEM((7, ROWS, FEATURES), jnp.bfloat16), pltpu.SemaphoreType.DMA((7,))],
    )
    own = within_team(packed)
    halo = to_next_team(own[1:, :NEAR], 1)
    crossing = swapped(own[:, FAR])
    out_s, own_s, back_s = attention(SELF, slots, own, halo)
    crossing, own_s = lax.optimization_barrier((crossing, own_s))
    out_c, own_c, back_c = attention(CROSS, slots, crossing, own, halo)
    home_s = to_next_team(back_s, -1)
    home_c = to_next_team(back_c, -1)
    joined = local_call(
        join_kernel,
        block_shape(TEAM, 4),
        vmem(6),
        (own_s, own_c, home_s, home_c, out_s, swapped(out_c)),
        "join",
    )
    outs = local_call(unpack_kernel, (flat,) * 7, vmem(1), (within_team(joined),), "unpack")
    return tuple(part[None] for part in outs)


def solution(mesh):
    rows = P("tower", ("dp", "ctx"), None)
    return jax.shard_map(
        body,
        mesh=mesh,
        in_specs=(rows,) * 7 + (P("ctx"),),
        out_specs=(rows,) * 7,
        check_vma=False,
    )
```

time: 650 us -> 128 us (0.20)
  the two profiles are of different devices: /device:TPU:38 before, /device:TPU:4 now
where the time goes in v1:
time: 128 us
  blocking collectives  42 us (33%)
  waiting for transfers between devices  38.4 us (30%)
  starting transfers between devices  33.1 us (26%)
  Pallas kernels  12.5 us (10%)
  between operations  1.37 us (1%)
    all_to_all x2, blocking collectives, within_team(): lax.all_to_all(value, 'ctx', 0, 0, axis_index_groups=teams, tiled=True)  42 us
    ppermute x2, waiting for transfers between devices, swapped(): return lax.ppermute(value, 'tower', [(0, 1), (1, 0)])  23.8 us
    ppermute x2, starting transfers between devices, swapped(): return lax.ppermute(value, 'tower', [(0, 1), (1, 0)])  16.7 us
    ppermute x3, starting transfers between devices, to_next_team(): return lax.ppermute(value, 'ctx', route)  16.4 us
    ppermute x3, waiting for transfers between devices, to_next_team(): return lax.ppermute(value, 'ctx', route)  14.5 us
    pallas_call x2, Pallas kernels, attention(): pl.pallas_call(kernel, out_shape=(block_shape(TEAM), block_shape(TEAM, dt...  9.65 us
    pallas_call x3, Pallas kernels, local_call(): pl.pallas_call(kernel, out_shape=out_shape, in_specs=in_specs, out_specs=...  2.89 us
  transfers between devices with their start and end apart: 5, of which 3 were waited for; matrix products, arithmetic and copies ran while one was open for 0% of the time, Pallas kernels for 4%

profile of v1, /device:TPU:4, one launch (start us, length us, event | category | flops | bytes accessed | tf_op | source)
XLA Modules:
  0.0 127.5 jit_solution(11361413884366190478)
XLA Ops:
  0.6 1.6 %pack.1 = bf16[8,4,128,128]{3,2,1,0:T(8,128)(2,1)S(1)} custom-call(bf16[128,512]{1,0:T(8,128)(2,1)} %bitcast.19, bf16[128,512]{1,0:T(8,128)(2,1)} %bitcast.20, bf16[128,512]{1,0:T(8,128)(2,1)} %bitcast.21, bf16[128,512]{1,0:T(8,128)(2,1)} %bitcast.22, bf16[128,512]{1,0:T(8,128)(2,1)} %bitcast.23, bf16[128,512]{1,0:T(8,128)(2,1)} %bitcast.24, ...), custom_call_target="tpu_custom_call" | custom-call | tf_op jit(solution)/shard_map/pack/pallas_call | solution.py:229
  2.2 20.7 %all_to_all.10.refs_1_.refs_2_ = bf16[8,4,128,128]{3,2,1,0:T(8,128)(2,1)S(1)} all-to-all(bf16[8,4,128,128]{3,2,1,0:T(8,128)(2,1)S(1)} %pack.1), channel_id=1, replica_groups={{0,2,4,6,8,10,12,14},{16,18,20,22,24,26,28,30},{32,34,36,38,40,42,44,46..., dimensions={0} | all-to-all | bytes 2097152 | tf_op jit(solution)/shard_map/all_to_all | solution.py:250
  22.9 3.2 %collective-permute-start.1 = (bf16[7,2,128,128]{3,2,1,0:T(8,128)(2,1)S(1)}, bf16[7,2,128,128]{3,2,1,0:T(8,128)(2,1)S(1)}, u32[]{:S(2)}, u32[]{:S(2)}) collective-permute-start(bf16[7,2,128,128]{3,2,1,0:T(8,128)(2,1)S(1)} %slice.9), channel_id=1, source_target_pairs={{0,24},{2,26},{4,28},{6,30},{8,16},{10,18},{12,20},{14,22},{16,40}... | collective-permute-start | bytes 1376264 | tf_op jit(solution)/shard_map/ppermute | solution.py:244
  26.2 14.8 %collective-permute-start = (bf16[8,128,128]{2,1,0:T(8,128)(2,1)S(1)}, bf16[8,128,128]{2,1,0:T(8,128)(2,1)S(1)}, u32[]{:S(2)}, u32[]{:S(2)}) collective-permute-start(bf16[8,128,128]{2,1,0:T(8,128)(2,1)S(1)} %slice_bitcast_fusion), channel_id=1, source_target_pairs={{0,256},{256,0},{1,257},{257,1},{2,258},{258,2},{3,259},{259,3},{4... | collective-permute-start | bytes 786440 | tf_op jit(solution)/shard_map/ppermute | solution.py:254
  41.7 0.1 pad_add_fusion.refs_0_
  41.7 0.0 collective-permute-done.1.refs_2_.refs_3_
  41.7 4.8 %attention_self.1 = (bf16[8,128,128]{2,1,0:T(8,128)(2,1)S(1)}, f32[8,128,128]{2,1,0:T(8,128)S(1)}, bf16[7,128,128]{2,1,0:T(8,128)(2,1)S(1)}) custom-call(s32[2]{0:T(128)S(1)} %pad_add_fusion.refs_0_, bf16[8,4,128,128]{3,2,1,0:T(8,128)(2,1)S(1)} %all_to_all.10.refs_1_.refs_2_, bf16[7,2,128,128]{3,2,1,0:T(8,128)(2,1)S(1)} %collective-permute-done.1.refs_2_.refs_3_), custom_call_target="tpu_custom_call" | custom-call | tf_op jit(solution)/shard_map/attention_self/pallas_call | solution.py:178
  46.6 23.8 %collective-permute-done.refs_1_ = bf16[8,128,128]{2,1,0:T(8,128)(2,1)S(1)} collective-permute-done((bf16[8,128,128]{2,1,0:T(8,128)(2,1)S(1)}, bf16[8,128,128]{2,1,0:T(8,128)(2,1)S(1)}, u32[]{:S(2)}, u32[]{:S(2)}) %collective-permute-start) | collective-permute-done | bytes 262176 | tf_op jit(solution)/shard_map/ppermute | solution.py:254
  70.4 4.8 %attention_cross.1 = (bf16[8,128,128]{2,1,0:T(8,128)(2,1)S(1)}, f32[8,128,128]{2,1,0:T(8,128)S(1)}, bf16[7,128,128]{2,1,0:T(8,128)(2,1)S(1)}) custom-call(s32[2]{0:T(128)S(1)} %pad_add_fusion.refs_0_, bf16[8,128,128]{2,1,0:T(8,128)(2,1)S(1)} %collective-permute-done.refs_1_, bf16[8,4,128,128]{3,2,1,0:T(8,128)(2,1)S(1)} %all_to_all.10.refs_1_.refs_2_, ...), custom_call_target="tpu_custom_call" | custom-call | tf_op jit(solution)/shard_map/attention_cross/pallas_call | solution.py:178
  75.2 1.9 %collective-permute-start.4 = (bf16[8,128,128]{2,1,0:T(8,128)(2,1)S(1)}, bf16[8,128,128]{2,1,0:T(8,128)(2,1)S(1)}, u32[]{:S(2)}, u32[]{:S(2)}) collective-permute-start(bf16[8,128,128]{2,1,0:T(8,128)(2,1)S(1)} %get-tuple-element.29), channel_id=1, source_target_pairs={{0,256},{256,0},{1,257},{257,1},{2,258},{258,2},{3,259},{259,3},{4... | collective-permute-start | bytes 786440 | tf_op jit(solution)/shard_map/ppermute | solution.py:254
  77.2 6.1 %collective-permute-start.3 = (bf16[7,128,128]{2,1,0:T(8,128)(2,1)S(1)}, bf16[7,128,128]{2,1,0:T(8,128)(2,1)S(1)}, u32[]{:S(2)}, u32[]{:S(2)}) collective-permute-start(bf16[7,128,128]{2,1,0:T(8,128)(2,1)S(1)} %get-tuple-element.27), channel_id=1, source_target_pairs={{0,248},{2,250},{4,252},{6,254},{8,240},{10,242},{12,244},{14,246}... | collective-permute-start | bytes 688136 | tf_op jit(solution)/shard_map/ppermute | solution.py:244
  83.2 7.1 %collective-permute-start.2 = (bf16[7,128,128]{2,1,0:T(8,128)(2,1)S(1)}, bf16[7,128,128]{2,1,0:T(8,128)(2,1)S(1)}, u32[]{:S(2)}, u32[]{:S(2)}) collective-permute-start(bf16[7,128,128]{2,1,0:T(8,128)(2,1)S(1)} %get-tuple-element.26), channel_id=1, source_target_pairs={{0,248},{2,250},{4,252},{6,254},{8,240},{10,242},{12,244},{14,246}... | collective-permute-start | bytes 688136 | tf_op jit(solution)/shard_map/ppermute | solution.py:244
  90.4 10.1 %collective-permute-done.3.home_c = bf16[7,128,128]{2,1,0:T(8,128)(2,1)S(1)} collective-permute-done((bf16[7,128,128]{2,1,0:T(8,128)(2,1)S(1)}, bf16[7,128,128]{2,1,0:T(8,128)(2,1)S(1)}, u32[]{:S(2)}, u32[]{:S(2)}) %collective-permute-start.3) | collective-permute-done | bytes 229408 | tf_op jit(solution)/shard_map/ppermute | solution.py:244
  100.5 4.4 %collective-permute-done.2.home_s = bf16[7,128,128]{2,1,0:T(8,128)(2,1)S(1)} collective-permute-done((bf16[7,128,128]{2,1,0:T(8,128)(2,1)S(1)}, bf16[7,128,128]{2,1,0:T(8,128)(2,1)S(1)}, u32[]{:S(2)}, u32[]{:S(2)}) %collective-permute-start.2) | collective-permute-done | bytes 229408 | tf_op jit(solution)/shard_map/ppermute | solution.py:244
  104.9 0.0 collective-permute-done.4.out_c
  104.9 0.1 join.1
  105.0 21.3 %all_to_all.11.parts = bf16[8,4,128,128]{3,2,1,0:T(8,128)(2,1)S(1)} all-to-all(bf16[8,4,128,128]{3,2,1,0:T(8,128)(2,1)S(1)} %join.1), channel_id=1, replica_groups={{0,2,4,6,8,10,12,14},{16,18,20,22,24,26,28,30},{32,34,36,38,40,42,44,46..., dimensions={0} | all-to-all | bytes 2097152 | tf_op jit(solution)/shard_map/all_to_all | solution.py:250
  126.3 1.2 unpack.1
  (2 shorter events, 0.0 us)
Async XLA Ops:
  22.9 18.8 %collective-permute-start.1 = (bf16[7,2,128,128]{3,2,1,0:T(8,128)(2,1)S(1)}, bf16[7,2,128,128]{3,2,1,0:T(8,128)(2,1)S(1)}, u32[]{:S(2)}, u32[]{:S(2)}) collective-permute-start(bf16[7,2,128,128]{3,2,1,0:T(8,128)(2,1)S(1)} %slice.9), channel_id=1, source_target_pairs={{0,24},{2,26},{4,28},{6,30},{8,16},{10,18},{12,20},{14,22},{16,40}... | collective-permute-start | bytes 1376264 | tf_op jit(solution)/shard_map/ppermute | solution.py:244
  26.2 44.2 %collective-permute-start = (bf16[8,128,128]{2,1,0:T(8,128)(2,1)S(1)}, bf16[8,128,128]{2,1,0:T(8,128)(2,1)S(1)}, u32[]{:S(2)}, u32[]{:S(2)}) collective-permute-start(bf16[8,128,128]{2,1,0:T(8,128)(2,1)S(1)} %slice_bitcast_fusion), channel_id=1, source_target_pairs={{0,256},{256,0},{1,257},{257,1},{2,258},{258,2},{3,259},{259,3},{4... | collective-permute-start | bytes 786440 | tf_op jit(solution)/shard_map/ppermute | solution.py:254
  75.2 29.6 %collective-permute-start.4 = (bf16[8,128,128]{2,1,0:T(8,128)(2,1)S(1)}, bf16[8,128,128]{2,1,0:T(8,128)(2,1)S(1)}, u32[]{:S(2)}, u32[]{:S(2)}) collective-permute-start(bf16[8,128,128]{2,1,0:T(8,128)(2,1)S(1)} %get-tuple-element.29), channel_id=1, source_target_pairs={{0,256},{256,0},{1,257},{257,1},{2,258},{258,2},{3,259},{259,3},{4... | collective-permute-start | bytes 786440 | tf_op jit(solution)/shard_map/ppermute | solution.py:254
  77.2 23.3 %collective-permute-start.3 = (bf16[7,128,128]{2,1,0:T(8,128)(2,1)S(1)}, bf16[7,128,128]{2,1,0:T(8,128)(2,1)S(1)}, u32[]{:S(2)}, u32[]{:S(2)}) collective-permute-start(bf16[7,128,128]{2,1,0:T(8,128)(2,1)S(1)} %get-tuple-element.27), channel_id=1, source_target_pairs={{0,248},{2,250},{4,252},{6,254},{8,240},{10,242},{12,244},{14,246}... | collective-permute-start | bytes 688136 | tf_op jit(solution)/shard_map/ppermute | solution.py:244
  83.2 21.6 %collective-permute-start.2 = (bf16[7,128,128]{2,1,0:T(8,128)(2,1)S(1)}, bf16[7,128,128]{2,1,0:T(8,128)(2,1)S(1)}, u32[]{:S(2)}, u32[]{:S(2)}) collective-permute-start(bf16[7,128,128]{2,1,0:T(8,128)(2,1)S(1)} %get-tuple-element.26), channel_id=1, source_target_pairs={{0,248},{2,250},{4,252},{6,254},{8,240},{10,242},{12,244},{14,246}... | collective-permute-start | bytes 688136 | tf_op jit(solution)/shard_map/ppermute | solution.py:244

commit v2 on v1

--- a/solution.py
+++ b/solution.py
@@ -42,7 +42,7 @@
 
 
 def pack_kernel(
-    query_s, key_s, value_s, query_c, key_c, value_c, upstream, out, held, arrived
+    query_s, key_s, value_s, query_c, key_c, value_c, upstream, far, near, held, arrived
 ):
     sources = (upstream, query_c, query_s, key_s, value_s, key_c, value_c)
     copies = [
@@ -58,7 +58,11 @@
         if right:
             copies[right].wait()
         for h in range(HEADS):
-            out[jnp.bitwise_xor(h, flip), kind] = paired(held.at[left], held.at[right], h)
+            value = paired(held.at[left], held.at[right], h)
+            if kind == FAR:
+                far[jnp.bitwise_xor(h, flip)] = value
+            else:
+                near[jnp.bitwise_xor(h, flip), kind] = value
 
 
 def attention_kernel(kind, slots, *refs):
@@ -262,19 +266,19 @@
     slots = jnp.stack([lax.rem(block_slot[0] - member + count, count), jnp.int32(count)])
     flat = jax.ShapeDtypeStruct((ROWS, FEATURES), jnp.bfloat16)
     inputs = (query_self, key_self, value_self, query_cross, key_cross, value_cross, cotangent)
-    packed = local_call(
+    far, near = local_call(
         pack_kernel,
-        block_shape(TEAM, 4),
+        (block_shape(TEAM), block_shape(TEAM, 3)),
         [pl.BlockSpec(memory_space=pltpu.HBM)] * 7,
         tuple(pltpu.with_memory_space_constraint(value[0], pltpu.HBM) for value in inputs),
         "pack",
         [pltpu.VMEM((7, ROWS, FEATURES), jnp.bfloat16), pltpu.SemaphoreType.DMA((7,))],
     )
-    own = within_team(packed)
+    arrived = swapped(far)
+    own = within_team(near)
     halo = to_next_team(own[1:, :NEAR], 1)
-    crossing = swapped(own[:, FAR])
+    crossing = within_team(arrived)
     out_s, own_s, back_s = attention(SELF, slots, own, halo)
-    crossing, own_s = lax.optimization_barrier((crossing, own_s))
     out_c, own_c, back_c = attention(CROSS, slots, crossing, own, halo)
     home_s = to_next_team(back_s, -1)
     home_c = to_next_team(back_c, -1)

time: 128 us -> 125 us (0.977)
  the two profiles are of different devices: /device:TPU:4 before, /device:TPU:2 now
where the time goes in v2:
time: 125 us; the launch traced here: 124 us
  starting transfers between devices  46.8 us (37%)
  waiting for transfers between devices  43.5 us (35%)
  blocking collectives  18.9 us (15%)
  Pallas kernels  13.4 us (11%)
  between operations  1.38 us (1%)
    ppermute x3, waiting for transfers between devices, to_next_team(): return lax.ppermute(value, 'ctx', route)  34.9 us
    ppermute x2, starting transfers between devices, swapped(): return lax.ppermute(value, 'tower', [(0, 1), (1, 0)])  21.4 us
    all_to_all x1, blocking collectives, within_team(): lax.all_to_all(value, 'ctx', 0, 0, axis_index_groups=teams, tiled=True)  18.9 us
    all_to_all x2, starting transfers between devices, within_team(): lax.all_to_all(value, 'ctx', 0, 0, axis_index_groups=teams, tiled=True)  15.1 us
    ppermute x3, starting transfers between devices, to_next_team(): return lax.ppermute(value, 'ctx', route)  10.3 us
    pallas_call x2, Pallas kernels, attention(): pl.pallas_call(kernel, out_shape=(block_shape(TEAM), block_shape(TEAM, dt...  9.66 us
    all_to_all x2, waiting for transfers between devices, within_team(): lax.all_to_all(value, 'ctx', 0, 0, axis_index_groups=teams, tiled=True)  5.09 us
    pallas_call x3, Pallas kernels, local_call(): pl.pallas_call(kernel, out_shape=out_shape, in_specs=in_specs, out_specs=...  3.79 us
  transfers between devices with their start and end apart: 7, of which 5 were waited for; matrix products, arithmetic and copies ran while one was open for 0% of the time, Pallas kernels for 4%

profile of v2, /device:TPU:2, one launch (start us, length us, event | category | flops | bytes accessed | tf_op | source)
XLA Modules:
  0.0 124.1 jit_solution(16962106766055348693)
XLA Ops:
  0.6 2.5 %pack.1 = (bf16[8,128,128]{2,1,0:T(8,128)(2,1)S(1)}, bf16[8,3,128,128]{3,2,1,0:T(8,128)(2,1)}) custom-call(bf16[128,512]{1,0:T(8,128)(2,1)} %bitcast.17, bf16[128,512]{1,0:T(8,128)(2,1)} %bitcast.18, bf16[128,512]{1,0:T(8,128)(2,1)} %bitcast.19, bf16[128,512]{1,0:T(8,128)(2,1)} %bitcast.20, bf16[128,512]{1,0:T(8,128)(2,1)} %bitcast.21, ...), custom_call_target="tpu_custom_call" | custom-call | tf_op jit(solution)/shard_map/pack/pallas_call | solution.py:233
  3.1 9.4 %all-to-all-start = ((bf16[8,3,128,128]{3,2,1,0:T(8,128)(2,1)}), bf16[8,3,128,128]{3,2,1,0:T(8,128)(2,1)S(1)}, u32[]{:S(2)}, u32[]{:S(2)}) async-start(bf16[8,3,128,128]{3,2,1,0:T(8,128)(2,1)} %get-tuple-element.22), calls=%async_computation | async-start | bytes 1572864 | tf_op jit(solution)/shard_map/all_to_all | solution.py:254
  12.5 12.3 %collective-permute-start.1 = (bf16[8,128,128]{2,1,0:T(8,128)(2,1)S(1)}, bf16[8,128,128]{2,1,0:T(8,128)(2,1)}, u32[]{:S(2)}, u32[]{:S(2)}) collective-permute-start(bf16[8,128,128]{2,1,0:T(8,128)(2,1)S(1)} %get-tuple-element.24), channel_id=1, source_target_pairs={{0,256},{256,0},{1,257},{257,1},{2,258},{258,2},{3,259},{259,3},{4... | collective-permute-start | bytes 786440 | tf_op jit(solution)/shard_map/ppermute | solution.py:258
  24.8 0.0 all-to-all-done.refs_1_.refs_2_
  24.8 2.6 %collective-permute-start = (bf16[7,2,128,128]{3,2,1,0:T(8,128)(2,1)S(1)}, bf16[7,2,128,128]{3,2,1,0:T(8,128)(2,1)S(1)}, u32[]{:S(2)}, u32[]{:S(2)}) collective-permute-start(bf16[7,2,128,128]{3,2,1,0:T(8,128)(2,1)S(1)} %slice.4), channel_id=1, source_target_pairs={{0,24},{2,26},{4,28},{6,30},{8,16},{10,18},{12,20},{14,22},{16,40}... | collective-permute-start | bytes 1376264 | tf_op jit(solution)/shard_map/ppermute | solution.py:248
  27.4 3.5 %collective-permute-done.1 = bf16[8,128,128]{2,1,0:T(8,128)(2,1)} collective-permute-done((bf16[8,128,128]{2,1,0:T(8,128)(2,1)S(1)}, bf16[8,128,128]{2,1,0:T(8,128)(2,1)}, u32[]{:S(2)}, u32[]{:S(2)}) %collective-permute-start.1) | collective-permute-done | bytes 262176 | tf_op jit(solution)/shard_map/ppermute | solution.py:258
  30.9 5.7 %all-to-all-start.1 = ((bf16[8,128,128]{2,1,0:T(8,128)(2,1)}), bf16[8,128,128]{2,1,0:T(8,128)(2,1)S(1)}, u32[]{:S(2)}, u32[]{:S(2)}) async-start(bf16[8,128,128]{2,1,0:T(8,128)(2,1)} %collective-permute-done.1), calls=%async_computation.1 | async-start | bytes 524288 | tf_op jit(solution)/shard_map/all_to_all | solution.py:254
  37.3 0.1 pad_add_fusion.refs_0_
  37.3 5.1 %all-to-all-done.1.refs_1_ = bf16[8,128,128]{2,1,0:T(8,128)(2,1)S(1)} async-done(((bf16[8,128,128]{2,1,0:T(8,128)(2,1)}), bf16[8,128,128]{2,1,0:T(8,128)(2,1)S(1)}, u32[]{:S(2)}, u32[]{:S(2)}) %all-to-all-start.1) | async-done | bytes 262176 | tf_op jit(solution)/shard_map/all_to_all | solution.py:254
  42.4 15.8 %collective-permute-done.refs_2_.refs_3_ = bf16[7,2,128,128]{3,2,1,0:T(8,128)(2,1)S(1)} collective-permute-done((bf16[7,2,128,128]{3,2,1,0:T(8,128)(2,1)S(1)}, bf16[7,2,128,128]{3,2,1,0:T(8,128)(2,1)S(1)}, u32[]{:S(2)}, u32[]{:S(2)}) %collective-permute-start) | collective-permute-done | bytes 458784 | tf_op jit(solution)/shard_map/ppermute | solution.py:248
  58.3 4.8 %attention_cross.1 = (bf16[8,128,128]{2,1,0:T(8,128)(2,1)S(1)}, f32[8,128,128]{2,1,0:T(8,128)S(1)}, bf16[7,128,128]{2,1,0:T(8,128)(2,1)S(1)}) custom-call(s32[2]{0:T(128)S(1)} %pad_add_fusion.refs_0_, bf16[8,128,128]{2,1,0:T(8,128)(2,1)S(1)} %all-to-all-done.1.refs_1_, bf16[8,3,128,128]{3,2,1,0:T(8,128)(2,1)S(1)} %all-to-all-done.refs_1_.refs_2_, ...), custom_call_target="tpu_custom_call" | custom-call | tf_op jit(solution)/shard_map/attention_cross/pallas_call | solution.py:182
  63.1 9.1 %collective-permute-start.4 = (bf16[8,128,128]{2,1,0:T(8,128)(2,1)S(1)}, bf16[8,128,128]{2,1,0:T(8,128)(2,1)S(1)}, u32[]{:S(2)}, u32[]{:S(2)}) collective-permute-start(bf16[8,128,128]{2,1,0:T(8,128)(2,1)S(1)} %get-tuple-element.29), channel_id=1, source_target_pairs={{0,256},{256,0},{1,257},{257,1},{2,258},{258,2},{3,259},{259,3},{4... | collective-permute-start | bytes 786440 | tf_op jit(solution)/shard_map/ppermute | solution.py:258
  72.2 5.8 %collective-permute-start.3 = (bf16[7,128,128]{2,1,0:T(8,128)(2,1)S(1)}, bf16[7,128,128]{2,1,0:T(8,128)(2,1)S(1)}, u32[]{:S(2)}, u32[]{:S(2)}) collective-permute-start(bf16[7,128,128]{2,1,0:T(8,128)(2,1)S(1)} %get-tuple-element.27), channel_id=1, source_target_pairs={{0,248},{2,250},{4,252},{6,254},{8,240},{10,242},{12,244},{14,246}... | collective-permute-start | bytes 688136 | tf_op jit(solution)/shard_map/ppermute | solution.py:248
  78.0 4.8 %attention_self.1 = (bf16[8,128,128]{2,1,0:T(8,128)(2,1)S(1)}, f32[8,128,128]{2,1,0:T(8,128)S(1)}, bf16[7,128,128]{2,1,0:T(8,128)(2,1)S(1)}) custom-call(s32[2]{0:T(128)S(1)} %pad_add_fusion.refs_0_, bf16[8,3,128,128]{3,2,1,0:T(8,128)(2,1)S(1)} %all-to-all-done.refs_1_.refs_2_, bf16[7,2,128,128]{3,2,1,0:T(8,128)(2,1)S(1)} %collective-permute-done.refs_2_.refs_3_), custom_call_target="tpu_custom_call" | custom-call | tf_op jit(solution)/shard_map/attention_self/pallas_call | solution.py:182
  82.9 1.9 %collective-permute-start.2 = (bf16[7,128,128]{2,1,0:T(8,128)(2,1)S(1)}, bf16[7,128,128]{2,1,0:T(8,128)(2,1)S(1)}, u32[]{:S(2)}, u32[]{:S(2)}) collective-permute-start(bf16[7,128,128]{2,1,0:T(8,128)(2,1)S(1)} %get-tuple-element.26), channel_id=1, source_target_pairs={{0,248},{2,250},{4,252},{6,254},{8,240},{10,242},{12,244},{14,246}... | collective-permute-start | bytes 688136 | tf_op jit(solution)/shard_map/ppermute | solution.py:248
  84.8 15.7 %collective-permute-done.3.home_c = bf16[7,128,128]{2,1,0:T(8,128)(2,1)S(1)} collective-permute-done((bf16[7,128,128]{2,1,0:T(8,128)(2,1)S(1)}, bf16[7,128,128]{2,1,0:T(8,128)(2,1)S(1)}, u32[]{:S(2)}, u32[]{:S(2)}) %collective-permute-start.3) | collective-permute-done | bytes 229408 | tf_op jit(solution)/shard_map/ppermute | solution.py:248
  100.5 3.4 %collective-permute-done.2.home_s = bf16[7,128,128]{2,1,0:T(8,128)(2,1)S(1)} collective-permute-done((bf16[7,128,128]{2,1,0:T(8,128)(2,1)S(1)}, bf16[7,128,128]{2,1,0:T(8,128)(2,1)S(1)}, u32[]{:S(2)}, u32[]{:S(2)}) %collective-permute-start.2) | collective-permute-done | bytes 229408 | tf_op jit(solution)/shard_map/ppermute | solution.py:248
  103.9 0.0 collective-permute-done.4.out_c
  103.9 0.1 join.1
  104.0 18.9 %all_to_all.15.parts = bf16[8,4,128,128]{3,2,1,0:T(8,128)(2,1)S(1)} all-to-all(bf16[8,4,128,128]{3,2,1,0:T(8,128)(2,1)S(1)} %join.1), channel_id=1, replica_groups={{0,2,4,6,8,10,12,14},{16,18,20,22,24,26,28,30},{32,34,36,38,40,42,44,46..., dimensions={0} | all-to-all | bytes 2097152 | tf_op jit(solution)/shard_map/all_to_all | solution.py:254
  122.9 1.2 unpack.1
  (1 shorter events, 0.0 us)
Async XLA Ops:
  3.1 21.7 %all-to-all-start = ((bf16[8,3,128,128]{3,2,1,0:T(8,128)(2,1)}), bf16[8,3,128,128]{3,2,1,0:T(8,128)(2,1)S(1)}, u32[]{:S(2)}, u32[]{:S(2)}) async-start(bf16[8,3,128,128]{3,2,1,0:T(8,128)(2,1)} %get-tuple-element.22), calls=%async_computation | async-start | bytes 1572864 | tf_op jit(solution)/shard_map/all_to_all | solution.py:254
  12.5 18.4 %collective-permute-start.1 = (bf16[8,128,128]{2,1,0:T(8,128)(2,1)S(1)}, bf16[8,128,128]{2,1,0:T(8,128)(2,1)}, u32[]{:S(2)}, u32[]{:S(2)}) collective-permute-start(bf16[8,128,128]{2,1,0:T(8,128)(2,1)S(1)} %get-tuple-element.24), channel_id=1, source_target_pairs={{0,256},{256,0},{1,257},{257,1},{2,258},{258,2},{3,259},{259,3},{4... | collective-permute-start | bytes 786440 | tf_op jit(solution)/shard_map/ppermute | solution.py:258
  24.8 33.5 %collective-permute-start = (bf16[7,2,128,128]{3,2,1,0:T(8,128)(2,1)S(1)}, bf16[7,2,128,128]{3,2,1,0:T(8,128)(2,1)S(1)}, u32[]{:S(2)}, u32[]{:S(2)}) collective-permute-start(bf16[7,2,128,128]{3,2,1,0:T(8,128)(2,1)S(1)} %slice.4), channel_id=1, source_target_pairs={{0,24},{2,26},{4,28},{6,30},{8,16},{10,18},{12,20},{14,22},{16,40}... | collective-permute-start | bytes 1376264 | tf_op jit(solution)/shard_map/ppermute | solution.py:248
  30.9 11.5 %all-to-all-start.1 = ((bf16[8,128,128]{2,1,0:T(8,128)(2,1)}), bf16[8,128,128]{2,1,0:T(8,128)(2,1)S(1)}, u32[]{:S(2)}, u32[]{:S(2)}) async-start(bf16[8,128,128]{2,1,0:T(8,128)(2,1)} %collective-permute-done.1), calls=%async_computation.1 | async-start | bytes 524288 | tf_op jit(solution)/shard_map/all_to_all | solution.py:254
  63.1 40.8 %collective-permute-start.4 = (bf16[8,128,128]{2,1,0:T(8,128)(2,1)S(1)}, bf16[8,128,128]{2,1,0:T(8,128)(2,1)S(1)}, u32[]{:S(2)}, u32[]{:S(2)}) collective-permute-start(bf16[8,128,128]{2,1,0:T(8,128)(2,1)S(1)} %get-tuple-element.29), channel_id=1, source_target_pairs={{0,256},{256,0},{1,257},{257,1},{2,258},{258,2},{3,259},{259,3},{4... | collective-permute-start | bytes 786440 | tf_op jit(solution)/shard_map/ppermute | solution.py:258
  72.2 28.3 %collective-permute-start.3 = (bf16[7,128,128]{2,1,0:T(8,128)(2,1)S(1)}, bf16[7,128,128]{2,1,0:T(8,128)(2,1)S(1)}, u32[]{:S(2)}, u32[]{:S(2)}) collective-permute-start(bf16[7,128,128]{2,1,0:T(8,128)(2,1)S(1)} %get-tuple-element.27), channel_id=1, source_target_pairs={{0,248},{2,250},{4,252},{6,254},{8,240},{10,242},{12,244},{14,246}... | collective-permute-start | bytes 688136 | tf_op jit(solution)/shard_map/ppermute | solution.py:248
  82.9 21.0 %collective-permute-start.2 = (bf16[7,128,128]{2,1,0:T(8,128)(2,1)S(1)}, bf16[7,128,128]{2,1,0:T(8,128)(2,1)S(1)}, u32[]{:S(2)}, u32[]{:S(2)}) collective-permute-start(bf16[7,128,128]{2,1,0:T(8,128)(2,1)S(1)} %get-tuple-element.26), channel_id=1, source_target_pairs={{0,248},{2,250},{4,252},{6,254},{8,240},{10,242},{12,244},{14,246}... | collective-permute-start | bytes 688136 | tf_op jit(solution)/shard_map/ppermute | solution.py:248

commit v3 on v2

--- a/solution.py
+++ b/solution.py
@@ -67,12 +67,21 @@
 
 def attention_kernel(kind, slots, *refs):
     if kind == SELF:
-        own, halo, out, dkv_own, dkv_halo, kv_t, scores, probs, stacks = refs
+        own, edge, out, dkv_own, dkv_halo, kv_t, scores, probs, stacks = refs
         queries = [own.at[b, NEAR] for b in range(TEAM)]
     else:
-        qdo, own, halo, out, dkv_own, dkv_halo, kv_t, scores, probs, stacks = refs
+        qdo, own, plane, below, out, dkv_own, dkv_halo, kv_t, scores, probs, stacks, edge = refs
         queries = [qdo.at[b] for b in range(TEAM)]
-    blocks = [halo.at[b, kind] for b in range(HALO)] + [own.at[b, kind] for b in range(TEAM)]
+
+        @pl.when(my_flip() == 0)
+        def _():
+            edge[...] = below[...]
+
+        @pl.when(my_flip() != 0)
+        def _():
+            edge[...] = plane[...]
+
+    blocks = [edge.at[b] for b in range(HALO)] + [own.at[b, kind] for b in range(TEAM)]
     first_half = lax.broadcasted_iota(jnp.int32, (ROWS, PAIR), 1) < HEAD
     causal = lax.broadcasted_iota(jnp.int32, (ROWS, ROWS), 0) <= lax.broadcasted_iota(
         jnp.int32, (ROWS, ROWS), 1
@@ -193,18 +202,30 @@
             pltpu.VMEM((2, GROUP, ROWS, BOTH), jnp.float32),
             pltpu.VMEM((SPAN, TEAM * BOTH), jnp.bfloat16),
             pltpu.VMEM((TEAM * BOTH, PAIR), jnp.bfloat16),
-        ],
+        ]
+        + [pltpu.VMEM((HALO, ROWS, PAIR), jnp.bfloat16)] * (kind == CROSS),
         compiler_params=pltpu.CompilerParams(vmem_limit_bytes=VMEM_BYTES),
         cost_estimate=pl.CostEstimate(flops=0, bytes_accessed=0, transcendentals=0),
         name="attention_cross" if kind == CROSS else "attention_self",
     )(*operands)
 
 
-def join_kernel(own_s, own_c, home_s, home_c, out_s, out_c, out):
-    for kind, own, home in ((SELF, own_s, home_s), (CROSS, own_c, home_c)):
+def join_kernel(own_s, own_c, home_s, plane, above, out_s, out_c, out):
+    def add(kind, own, home):
         out[0, kind] = own[0].astype(jnp.bfloat16)
         for b in range(HALO):
             out[b + 1, kind] = (own[b + 1] + home[b].astype(jnp.float32)).astype(jnp.bfloat16)
+
+    add(SELF, own_s, home_s)
+
+    @pl.when(my_flip() == 0)
+    def _():
+        add(CROSS, own_c, plane)
+
+    @pl.when(my_flip() != 0)
+    def _():
+        add(CROSS, own_c, above)
+
     for b in range(TEAM):
         out[b, NEAR] = out_s[b]
         out[b, FAR] = out_c[b]
@@ -246,6 +267,17 @@
     count = lax.axis_size("ctx")
     route = [(i, (i + step * TEAM) % count ^ (TEAM // 2)) for i in range(count)]
     return lax.ppermute(value, "ctx", route)
+
+
+def in_plane(value):
+    count = lax.axis_size("ctx")
+    return lax.ppermute(value, "ctx", [(i, i ^ (TEAM + TEAM // 2)) for i in range(count)])
+
+
+def to_next_plane(value, step, odd):
+    count = lax.axis_size("ctx")
+    senders = [i for i in range(count) if i // TEAM % 2 == odd]
+    return lax.ppermute(value, "ctx", [(i, (i + step * 2 * TEAM) % count) for i in senders])
 
 
 def within_team(value):
@@ -276,17 +308,20 @@
     )
     arrived = swapped(far)
     own = within_team(near)
-    halo = to_next_team(own[1:, :NEAR], 1)
+    halo = to_next_team(own[1:, SELF], 1)
+    plane = in_plane(own[1:, CROSS])
+    below = to_next_plane(plane, 1, 0)
     crossing = within_team(arrived)
     out_s, own_s, back_s = attention(SELF, slots, own, halo)
-    out_c, own_c, back_c = attention(CROSS, slots, crossing, own, halo)
+    out_c, own_c, back_c = attention(CROSS, slots, crossing, own, plane, below)
     home_s = to_next_team(back_s, -1)
-    home_c = to_next_team(back_c, -1)
+    home_c = in_plane(back_c)
+    above = to_next_plane(home_c, -1, 1)
     joined = local_call(
         join_kernel,
         block_shape(TEAM, 4),
-        vmem(6),
-        (own_s, own_c, home_s, home_c, out_s, swapped(out_c)),
+        vmem(7),
+        (own_s, own_c, home_s, home_c, above, out_s, swapped(out_c)),
         "join",
     )
     outs = local_call(unpack_kernel, (flat,) * 7, vmem(1), (within_team(joined),), "unpack")

time: 125 us -> 128 us (1.024)
  the two profiles are of different devices: /device:TPU:2 before, /device:TPU:36 now
where the time goes in v3:
time: 128 us; the launch traced here: 127 us
  starting transfers between devices  51.5 us (40%)
  waiting for transfers between devices  40 us (31%)
  blocking collectives  20.5 us (16%)
  Pallas kernels  13.5 us (11%)
  between operations  1.42 us (1%)
    ppermute x2, starting transfers between devices, swapped(): return lax.ppermute(value, 'tower', [(0, 1), (1, 0)])  26.9 us
    all_to_all x1, blocking collectives, within_team(): lax.all_to_all(value, 'ctx', 0, 0, axis_index_groups=teams, tiled=True)  20.5 us
    ppermute x2, waiting for transfers between devices, swapped(): return lax.ppermute(value, 'tower', [(0, 1), (1, 0)])  19.9 us
    ppermute x2, waiting for transfers between devices, to_next_team(): return lax.ppermute(value, 'ctx', route)  14.1 us
    all_to_all x2, starting transfers between devices, within_team(): lax.all_to_all(value, 'ctx', 0, 0, axis_index_groups=teams, tiled=True)  10.5 us
    pallas_call x2, Pallas kernels, attention(): pl.pallas_call(kernel, out_shape=(block_shape(TEAM), block_shape(TEAM, dt...  9.71 us
    ppermute x2, starting transfers between devices, in_plane(): lax.ppermute(value, 'ctx', [(i, i ^ TEAM + TEAM // 2) for i in range(coun...  7.21 us
    all_to_all x2, waiting for transfers between devices, within_team(): lax.all_to_all(value, 'ctx', 0, 0, axis_index_groups=teams, tiled=True)  3.89 us
  transfers between devices with their start and end apart: 10, of which 4 were waited for; matrix products, arithmetic and copies ran while one was open for 0% of the time, Pallas kernels for 8%

profile of v3, /device:TPU:36, one launch (start us, length us, event | category | flops | bytes accessed | tf_op | source)
XLA Modules:
  0.0 127.1 jit_solution(10865434192928774884)
XLA Ops:
  0.6 2.5 %pack.1 = (bf16[8,128,128]{2,1,0:T(8,128)(2,1)S(1)}, bf16[8,3,128,128]{3,2,1,0:T(8,128)(2,1)}) custom-call(bf16[128,512]{1,0:T(8,128)(2,1)} %bitcast.25, bf16[128,512]{1,0:T(8,128)(2,1)} %bitcast.26, bf16[128,512]{1,0:T(8,128)(2,1)} %bitcast.27, bf16[128,512]{1,0:T(8,128)(2,1)} %bitcast.28, bf16[128,512]{1,0:T(8,128)(2,1)} %bitcast.29, ...), custom_call_target="tpu_custom_call" | custom-call | tf_op jit(solution)/shard_map/pack/pallas_call | solution.py:254
  3.1 5.1 %all-to-all-start = ((bf16[8,3,128,128]{3,2,1,0:T(8,128)(2,1)}), bf16[8,3,128,128]{3,2,1,0:T(8,128)(2,1)S(1)}, u32[]{:S(2)}, u32[]{:S(2)}) async-start(bf16[8,3,128,128]{3,2,1,0:T(8,128)(2,1)} %get-tuple-element.22), calls=%async_computation | async-start | bytes 1572864 | tf_op jit(solution)/shard_map/all_to_all | solution.py:286
  8.2 14.8 %collective-permute-start.1 = (bf16[8,128,128]{2,1,0:T(8,128)(2,1)S(1)}, bf16[8,128,128]{2,1,0:T(8,128)(2,1)}, u32[]{:S(2)}, u32[]{:S(2)}) collective-permute-start(bf16[8,128,128]{2,1,0:T(8,128)(2,1)S(1)} %get-tuple-element.24), channel_id=1, source_target_pairs={{0,256},{256,0},{1,257},{257,1},{2,258},{258,2},{3,259},{259,3},{4... | collective-permute-start | bytes 786440 | tf_op jit(solution)/shard_map/ppermute | solution.py:290
  23.1 0.0 all-to-all-done.refs_1_.refs_2_
  23.1 3.3 %collective-permute-start.2 = (bf16[7,128,128]{2,1,0:T(8,128)(2,1)S(1)}, bf16[7,128,128]{2,1,0:T(8,128)(2,1)S(1)}, u32[]{:S(2)}, u32[]{:S(2)}) collective-permute-start(bf16[7,128,128]{2,1,0:T(8,128)(2,1)S(1)} %get-tuple-element.37), channel_id=1, source_target_pairs={{0,24},{2,26},{4,28},{6,30},{8,16},{10,18},{12,20},{14,22},{16,8},... | collective-permute-start | bytes 688136 | tf_op jit(solution)/shard_map/ppermute | solution.py:274
  26.4 19.9 %collective-permute-done.1 = bf16[8,128,128]{2,1,0:T(8,128)(2,1)} collective-permute-done((bf16[8,128,128]{2,1,0:T(8,128)(2,1)S(1)}, bf16[8,128,128]{2,1,0:T(8,128)(2,1)}, u32[]{:S(2)}, u32[]{:S(2)}) %collective-permute-start.1) | collective-permute-done | bytes 262176 | tf_op jit(solution)/shard_map/ppermute | solution.py:290
  46.3 5.4 %all-to-all-start.1 = ((bf16[8,128,128]{2,1,0:T(8,128)(2,1)}), bf16[8,128,128]{2,1,0:T(8,128)(2,1)S(1)}, u32[]{:S(2)}, u32[]{:S(2)}) async-start(bf16[8,128,128]{2,1,0:T(8,128)(2,1)} %collective-permute-done.1), calls=%async_computation.1 | async-start | bytes 524288 | tf_op jit(solution)/shard_map/all_to_all | solution.py:286
  51.7 0.0 collective-permute-done.2.refs_3_
  51.7 0.7 collective-permute-start.3
  53.0 0.1 pad_add_fusion.refs_0_
  53.1 1.9 %collective-permute-start = (bf16[7,128,128]{2,1,0:T(8,128)(2,1)S(1)}, bf16[7,128,128]{2,1,0:T(8,128)(2,1)S(1)}, u32[]{:S(2)}, u32[]{:S(2)}) collective-permute-start(bf16[7,128,128]{2,1,0:T(8,128)(2,1)S(1)} %get-tuple-element.38), channel_id=1, source_target_pairs={{0,24},{2,26},{4,28},{6,30},{8,16},{10,18},{12,20},{14,22},{16,40}... | collective-permute-start | bytes 688136 | tf_op jit(solution)/shard_map/ppermute | solution.py:269
  55.0 3.9 %all-to-all-done.1.refs_1_ = bf16[8,128,128]{2,1,0:T(8,128)(2,1)S(1)} async-done(((bf16[8,128,128]{2,1,0:T(8,128)(2,1)}), bf16[8,128,128]{2,1,0:T(8,128)(2,1)S(1)}, u32[]{:S(2)}, u32[]{:S(2)}) %all-to-all-start.1) | async-done | bytes 262176 | tf_op jit(solution)/shard_map/all_to_all | solution.py:286
  58.9 4.9 %attention_cross.1 = (bf16[8,128,128]{2,1,0:T(8,128)(2,1)S(1)}, f32[8,128,128]{2,1,0:T(8,128)S(1)}, bf16[7,128,128]{2,1,0:T(8,128)(2,1)S(1)}) custom-call(s32[2]{0:T(128)S(1)} %pad_add_fusion.refs_0_, bf16[8,128,128]{2,1,0:T(8,128)(2,1)S(1)} %all-to-all-done.1.refs_1_, bf16[8,3,128,128]{3,2,1,0:T(8,128)(2,1)S(1)} %all-to-all-done.refs_1_.refs_2_, ...), custom_call_target="tpu_custom_call" | custom-call | tf_op jit(solution)/shard_map/attention_cross/pallas_call | solution.py:191
  63.8 3.9 %collective-permute-start.5 = (bf16[7,128,128]{2,1,0:T(8,128)(2,1)S(1)}, bf16[7,128,128]{2,1,0:T(8,128)(2,1)S(1)}, u32[]{:S(2)}, u32[]{:S(2)}) collective-permute-start(bf16[7,128,128]{2,1,0:T(8,128)(2,1)S(1)} %get-tuple-element.27), channel_id=1, source_target_pairs={{0,24},{2,26},{4,28},{6,30},{8,16},{10,18},{12,20},{14,22},{16,8},... | collective-permute-start | bytes 688136 | tf_op jit(solution)/shard_map/ppermute | solution.py:274
  67.7 12.1 %collective-permute-start.7 = (bf16[8,128,128]{2,1,0:T(8,128)(2,1)S(1)}, bf16[8,128,128]{2,1,0:T(8,128)(2,1)S(1)}, u32[]{:S(2)}, u32[]{:S(2)}) collective-permute-start(bf16[8,128,128]{2,1,0:T(8,128)(2,1)S(1)} %get-tuple-element.29), channel_id=1, source_target_pairs={{0,256},{256,0},{1,257},{257,1},{2,258},{258,2},{3,259},{259,3},{4... | collective-permute-start | bytes 786440 | tf_op jit(solution)/shard_map/ppermute | solution.py:290
  79.9 4.8 %attention_self.1 = (bf16[8,128,128]{2,1,0:T(8,128)(2,1)S(1)}, f32[8,128,128]{2,1,0:T(8,128)S(1)}, bf16[7,128,128]{2,1,0:T(8,128)(2,1)S(1)}) custom-call(s32[2]{0:T(128)S(1)} %pad_add_fusion.refs_0_, bf16[8,3,128,128]{3,2,1,0:T(8,128)(2,1)S(1)} %all-to-all-done.refs_1_.refs_2_, bf16[7,128,128]{2,1,0:T(8,128)(2,1)S(1)} %collective-permute-done.refs_2_), custom_call_target="tpu_custom_call" | custom-call | tf_op jit(solution)/shard_map/attention_self/pallas_call | solution.py:191
  84.7 1.9 %collective-permute-start.4 = (bf16[7,128,128]{2,1,0:T(8,128)(2,1)S(1)}, bf16[7,128,128]{2,1,0:T(8,128)(2,1)S(1)}, u32[]{:S(2)}, u32[]{:S(2)}) collective-permute-start(bf16[7,128,128]{2,1,0:T(8,128)(2,1)S(1)} %get-tuple-element.26), channel_id=1, source_target_pairs={{0,248},{2,250},{4,252},{6,254},{8,240},{10,242},{12,244},{14,246}... | collective-permute-start | bytes 688136 | tf_op jit(solution)/shard_map/ppermute | solution.py:269
  86.7 2.4 %collective-permute-start.6 = (bf16[7,128,128]{2,1,0:T(8,128)(2,1)S(1)}, bf16[7,128,128]{2,1,0:T(8,128)(2,1)S(1)}, u32[]{:S(2)}, u32[]{:S(2)}) collective-permute-start(bf16[7,128,128]{2,1,0:T(8,128)(2,1)S(1)} %collective-permute-done.5.plane), channel_id=1, source_target_pairs={{16,240},{18,242},{20,244},{22,246},{24,248},{26,250},{28,252},{30... | collective-permute-start | bytes 688136 | tf_op jit(solution)/shard_map/ppermute | solution.py:280
  89.0 14.1 %collective-permute-done.4.home_s = bf16[7,128,128]{2,1,0:T(8,128)(2,1)S(1)} collective-permute-done((bf16[7,128,128]{2,1,0:T(8,128)(2,1)S(1)}, bf16[7,128,128]{2,1,0:T(8,128)(2,1)S(1)}, u32[]{:S(2)}, u32[]{:S(2)}) %collective-permute-start.4) | collective-permute-done | bytes 229408 | tf_op jit(solution)/shard_map/ppermute | solution.py:269
  103.1 0.0 collective-permute-done.7.out_c
  103.1 2.1 %collective-permute-done.6.above = bf16[7,128,128]{2,1,0:T(8,128)(2,1)S(1)} collective-permute-done((bf16[7,128,128]{2,1,0:T(8,128)(2,1)S(1)}, bf16[7,128,128]{2,1,0:T(8,128)(2,1)S(1)}, u32[]{:S(2)}, u32[]{:S(2)}) %collective-permute-start.6) | collective-permute-done | bytes 229408 | tf_op jit(solution)/shard_map/ppermute | solution.py:280
  105.2 0.1 join.1
  105.3 20.5 %all_to_all.15.parts = bf16[8,4,128,128]{3,2,1,0:T(8,128)(2,1)S(1)} all-to-all(bf16[8,4,128,128]{3,2,1,0:T(8,128)(2,1)S(1)} %join.1), channel_id=1, replica_groups={{0,2,4,6,8,10,12,14},{16,18,20,22,24,26,28,30},{32,34,36,38,40,42,44,46..., dimensions={0} | all-to-all | bytes 2097152 | tf_op jit(solution)/shard_map/all_to_all | solution.py:286
  125.9 1.2 unpack.1
  (4 shorter events, 0.0 us)
Async XLA Ops:
  3.1 19.9 %all-to-all-start = ((bf16[8,3,128,128]{3,2,1,0:T(8,128)(2,1)}), bf16[8,3,128,128]{3,2,1,0:T(8,128)(2,1)S(1)}, u32[]{:S(2)}, u32[]{:S(2)}) async-start(bf16[8,3,128,128]{3,2,1,0:T(8,128)(2,1)} %get-tuple-element.22), calls=%async_computation | async-start | bytes 1572864 | tf_op jit(solution)/shard_map/all_to_all | solution.py:286
  8.2 38.0 %collective-permute-start.1 = (bf16[8,128,128]{2,1,0:T(8,128)(2,1)S(1)}, bf16[8,128,128]{2,1,0:T(8,128)(2,1)}, u32[]{:S(2)}, u32[]{:S(2)}) collective-permute-start(bf16[8,128,128]{2,1,0:T(8,128)(2,1)S(1)} %get-tuple-element.24), channel_id=1, source_target_pairs={{0,256},{256,0},{1,257},{257,1},{2,258},{258,2},{3,259},{259,3},{4... | collective-permute-start | bytes 786440 | tf_op jit(solution)/shard_map/ppermute | solution.py:290
  23.1 28.6 %collective-permute-start.2 = (bf16[7,128,128]{2,1,0:T(8,128)(2,1)S(1)}, bf16[7,128,128]{2,1,0:T(8,128)(2,1)S(1)}, u32[]{:S(2)}, u32[]{:S(2)}) collective-permute-start(bf16[7,128,128]{2,1,0:T(8,128)(2,1)S(1)} %get-tuple-element.37), channel_id=1, source_target_pairs={{0,24},{2,26},{4,28},{6,30},{8,16},{10,18},{12,20},{14,22},{16,8},... | collective-permute-start | bytes 688136 | tf_op jit(solution)/shard_map/ppermute | solution.py:274
  46.3 12.6 %all-to-all-start.1 = ((bf16[8,128,128]{2,1,0:T(8,128)(2,1)}), bf16[8,128,128]{2,1,0:T(8,128)(2,1)S(1)}, u32[]{:S(2)}, u32[]{:S(2)}) async-start(bf16[8,128,128]{2,1,0:T(8,128)(2,1)} %collective-permute-done.1), calls=%async_computation.1 | async-start | bytes 524288 | tf_op jit(solution)/shard_map/all_to_all | solution.py:286
  51.7 7.2 %collective-permute-start.3 = (bf16[7,128,128]{2,1,0:T(8,128)(2,1)S(1)}, bf16[7,128,128]{2,1,0:T(8,128)(2,1)S(1)}, u32[]{:S(2)}, u32[]{:S(2)}) collective-permute-start(bf16[7,128,128]{2,1,0:T(8,128)(2,1)S(1)} %collective-permute-done.2.refs_3_), channel_id=1, source_target_pairs={{0,32},{2,34},{4,36},{6,38},{8,40},{10,42},{12,44},{14,46},{32,64}... | collective-permute-start | bytes 688136 | tf_op jit(solution)/shard_map/ppermute | solution.py:280
  53.1 26.8 %collective-permute-start = (bf16[7,128,128]{2,1,0:T(8,128)(2,1)S(1)}, bf16[7,128,128]{2,1,0:T(8,128)(2,1)S(1)}, u32[]{:S(2)}, u32[]{:S(2)}) collective-permute-start(bf16[7,128,128]{2,1,0:T(8,128)(2,1)S(1)} %get-tuple-element.38), channel_id=1, source_target_pairs={{0,24},{2,26},{4,28},{6,30},{8,16},{10,18},{12,20},{14,22},{16,40}... | collective-permute-start | bytes 688136 | tf_op jit(solution)/shard_map/ppermute | solution.py:269
  63.8 22.9 %collective-permute-start.5 = (bf16[7,128,128]{2,1,0:T(8,128)(2,1)S(1)}, bf16[7,128,128]{2,1,0:T(8,128)(2,1)S(1)}, u32[]{:S(2)}, u32[]{:S(2)}) collective-permute-start(bf16[7,128,128]{2,1,0:T(8,128)(2,1)S(1)} %get-tuple-element.27), channel_id=1, source_target_pairs={{0,24},{2,26},{4,28},{6,30},{8,16},{10,18},{12,20},{14,22},{16,8},... | collective-permute-start | bytes 688136 | tf_op jit(solution)/shard_map/ppermute | solution.py:274
  67.7 35.4 %collective-permute-start.7 = (bf16[8,128,128]{2,1,0:T(8,128)(2,1)S(1)}, bf16[8,128,128]{2,1,0:T(8,128)(2,1)S(1)}, u32[]{:S(2)}, u32[]{:S(2)}) collective-permute-start(bf16[8,128,128]{2,1,0:T(8,128)(2,1)S(1)} %get-tuple-element.29), channel_id=1, source_target_pairs={{0,256},{256,0},{1,257},{257,1},{2,258},{258,2},{3,259},{259,3},{4... | collective-permute-start | bytes 786440 | tf_op jit(solution)/shard_map/ppermute | solution.py:290
  84.7 18.4 %collective-permute-start.4 = (bf16[7,128,128]{2,1,0:T(8,128)(2,1)S(1)}, bf16[7,128,128]{2,1,0:T(8,128)(2,1)S(1)}, u32[]{:S(2)}, u32[]{:S(2)}) collective-permute-start(bf16[7,128,128]{2,1,0:T(8,128)(2,1)S(1)} %get-tuple-element.26), channel_id=1, source_target_pairs={{0,248},{2,250},{4,252},{6,254},{8,240},{10,242},{12,244},{14,246}... | collective-permute-start | bytes 688136 | tf_op jit(solution)/shard_map/ppermute | solution.py:269
  86.7 18.5 %collective-permute-start.6 = (bf16[7,128,128]{2,1,0:T(8,128)(2,1)S(1)}, bf16[7,128,128]{2,1,0:T(8,128)(2,1)S(1)}, u32[]{:S(2)}, u32[]{:S(2)}) collective-permute-start(bf16[7,128,128]{2,1,0:T(8,128)(2,1)S(1)} %collective-permute-done.5.plane), channel_id=1, source_target_pairs={{16,240},{18,242},{20,244},{22,246},{24,248},{26,250},{28,252},{30... | collective-permute-start | bytes 688136 | tf_op jit(solution)/shard_map/ppermute | solution.py:280

commit v4 on v2

--- a/solution.py
+++ b/solution.py
@@ -72,7 +72,7 @@
     else:
         qdo, own, halo, out, dkv_own, dkv_halo, kv_t, scores, probs, stacks = refs
         queries = [qdo.at[b] for b in range(TEAM)]
-    blocks = [halo.at[b, kind] for b in range(HALO)] + [own.at[b, kind] for b in range(TEAM)]
+    blocks = [halo.at[b] for b in range(HALO)] + [own.at[b, kind] for b in range(TEAM)]
     first_half = lax.broadcasted_iota(jnp.int32, (ROWS, PAIR), 1) < HEAD
     causal = lax.broadcasted_iota(jnp.int32, (ROWS, ROWS), 0) <= lax.broadcasted_iota(
         jnp.int32, (ROWS, ROWS), 1
@@ -200,14 +200,13 @@
     )(*operands)
 
 
-def join_kernel(own_s, own_c, home_s, home_c, out_s, out_c, out):
+def join_kernel(own_s, own_c, home_s, home_c, out_c, out):
     for kind, own, home in ((SELF, own_s, home_s), (CROSS, own_c, home_c)):
         out[0, kind] = own[0].astype(jnp.bfloat16)
         for b in range(HALO):
             out[b + 1, kind] = (own[b + 1] + home[b].astype(jnp.float32)).astype(jnp.bfloat16)
     for b in range(TEAM):
-        out[b, NEAR] = out_s[b]
-        out[b, FAR] = out_c[b]
+        out[b, NEAR] = out_c[b]
 
 
 def halves(first, second):
@@ -216,15 +215,16 @@
     return left, right
 
 
-def unpack_kernel(parts, attended, query_s, key_s, value_s, query_c, key_c, value_c):
+def unpack_kernel(parts, parts_s, attended, query_s, key_s, value_s, query_c, key_c, value_c):
     flip = my_flip()
     for h in range(0, HEADS, 2):
         lanes = pl.ds(h * HEAD, PAIR)
-        first, second = parts.at[jnp.bitwise_xor(h, flip)], parts.at[jnp.bitwise_xor(h + 1, flip)]
+        left, right = jnp.bitwise_xor(h, flip), jnp.bitwise_xor(h + 1, flip)
+        first, second = parts.at[left], parts.at[right]
         key_s[:, lanes], value_s[:, lanes] = halves(first[SELF], second[SELF])
         key_c[:, lanes], value_c[:, lanes] = halves(first[CROSS], second[CROSS])
-        query_s[:, lanes], near = halves(first[NEAR], second[NEAR])
-        query_c[:, lanes], far = halves(first[FAR], second[FAR])
+        query_s[:, lanes], near = halves(parts_s[left], parts_s[right])
+        query_c[:, lanes], far = halves(first[NEAR], second[NEAR])
         total = near.astype(jnp.float32) + far.astype(jnp.float32)
         attended[:, lanes] = total.astype(jnp.bfloat16)
 
@@ -276,20 +276,24 @@
     )
     arrived = swapped(far)
     own = within_team(near)
-    halo = to_next_team(own[1:, :NEAR], 1)
+    halo_c = to_next_team(own[1:, CROSS], 1)
+    halo_s = to_next_team(own[1:, SELF], 1)
     crossing = within_team(arrived)
-    out_s, own_s, back_s = attention(SELF, slots, own, halo)
-    out_c, own_c, back_c = attention(CROSS, slots, crossing, own, halo)
+    out_s, own_s, back_s = attention(SELF, slots, own, halo_s)
+    out_c, own_c, back_c = attention(CROSS, slots, crossing, own, halo_c)
     home_s = to_next_team(back_s, -1)
     home_c = to_next_team(back_c, -1)
     joined = local_call(
         join_kernel,
-        block_shape(TEAM, 4),
-        vmem(6),
-        (own_s, own_c, home_s, home_c, out_s, swapped(out_c)),
+        block_shape(TEAM, 3),
+        vmem(5),
+        (own_s, own_c, home_s, home_c, swapped(out_c)),
         "join",
     )
-    outs = local_call(unpack_kernel, (flat,) * 7, vmem(1), (within_team(joined),), "unpack")
+    parts_s = within_team(out_s)
+    outs = local_call(
+        unpack_kernel, (flat,) * 7, vmem(2), (within_team(joined), parts_s), "unpack"
+    )
     return tuple(part[None] for part in outs)
 
 

time: 125 us -> 127 us (1.016)
  the two profiles are of different devices: /device:TPU:2 before, /device:TPU:36 now
where the time goes in v4:
time: 127 us
  starting transfers between devices  52.4 us (41%)
  waiting for transfers between devices  39.4 us (31%)
  blocking collectives  19.3 us (15%)
  Pallas kernels  14.1 us (11%)
  between operations  1.39 us (1%)
    ppermute x2, starting transfers between devices, swapped(): return lax.ppermute(value, 'tower', [(0, 1), (1, 0)])  26.9 us
    ppermute x2, waiting for transfers between devices, swapped(): return lax.ppermute(value, 'tower', [(0, 1), (1, 0)])  23.2 us
    all_to_all x1, blocking collectives, within_team(): lax.all_to_all(value, 'ctx', 0, 0, axis_index_groups=teams, tiled=True)  19.3 us
    all_to_all x3, starting transfers between devices, within_team(): lax.all_to_all(value, 'ctx', 0, 0, axis_index_groups=teams, tiled=True)  15.6 us
    ppermute x4, waiting for transfers between devices, to_next_team(): return lax.ppermute(value, 'ctx', route)  13.6 us
    pallas_call x2, Pallas kernels, attention(): pl.pallas_call(kernel, out_shape=(block_shape(TEAM), block_shape(TEAM, dt...  10.3 us
    ppermute x4, starting transfers between devices, to_next_team(): return lax.ppermute(value, 'ctx', route)  9.83 us
    pallas_call x3, Pallas kernels, local_call(): pl.pallas_call(kernel, out_shape=out_shape, in_specs=in_specs, out_specs=...  3.77 us
  transfers between devices with their start and end apart: 9, of which 5 were waited for; matrix products, arithmetic and copies ran while one was open for 0% of the time, Pallas kernels for 8%

profile of v4, /device:TPU:36, one launch (start us, length us, event | category | flops | bytes accessed | tf_op | source)
XLA Modules:
  0.0 126.6 jit_solution(10184213644798025285)
XLA Ops:
  0.6 2.5 %pack.1 = (bf16[8,128,128]{2,1,0:T(8,128)(2,1)S(1)}, bf16[8,3,128,128]{3,2,1,0:T(8,128)(2,1)}) custom-call(bf16[128,512]{1,0:T(8,128)(2,1)} %bitcast.25, bf16[128,512]{1,0:T(8,128)(2,1)} %bitcast.26, bf16[128,512]{1,0:T(8,128)(2,1)} %bitcast.27, bf16[128,512]{1,0:T(8,128)(2,1)} %bitcast.28, bf16[128,512]{1,0:T(8,128)(2,1)} %bitcast.29, ...), custom_call_target="tpu_custom_call" | custom-call | tf_op jit(solution)/shard_map/pack/pallas_call | solution.py:233
  3.1 5.1 %all-to-all-start = ((bf16[8,3,128,128]{3,2,1,0:T(8,128)(2,1)}), bf16[8,3,128,128]{3,2,1,0:T(8,128)(2,1)S(1)}, u32[]{:S(2)}, u32[]{:S(2)}) async-start(bf16[8,3,128,128]{3,2,1,0:T(8,128)(2,1)} %get-tuple-element.22), calls=%async_computation | async-start | bytes 1572864 | tf_op jit(solution)/shard_map/all_to_all | solution.py:254
  8.2 14.8 %collective-permute-start.1 = (bf16[8,128,128]{2,1,0:T(8,128)(2,1)S(1)}, bf16[8,128,128]{2,1,0:T(8,128)(2,1)}, u32[]{:S(2)}, u32[]{:S(2)}) collective-permute-start(bf16[8,128,128]{2,1,0:T(8,128)(2,1)S(1)} %get-tuple-element.24), channel_id=1, source_target_pairs={{0,256},{256,0},{1,257},{257,1},{2,258},{258,2},{3,259},{259,3},{4... | collective-permute-start | bytes 786440 | tf_op jit(solution)/shard_map/ppermute | solution.py:258
  23.1 23.2 %collective-permute-done.1 = bf16[8,128,128]{2,1,0:T(8,128)(2,1)} collective-permute-done((bf16[8,128,128]{2,1,0:T(8,128)(2,1)S(1)}, bf16[8,128,128]{2,1,0:T(8,128)(2,1)}, u32[]{:S(2)}, u32[]{:S(2)}) %collective-permute-start.1) | collective-permute-done | bytes 262176 | tf_op jit(solution)/shard_map/ppermute | solution.py:258
  46.3 0.0 all-to-all-done.refs_1_.refs_2_
  46.3 5.4 %all-to-all-start.1 = ((bf16[8,128,128]{2,1,0:T(8,128)(2,1)}), bf16[8,128,128]{2,1,0:T(8,128)(2,1)S(1)}, u32[]{:S(2)}, u32[]{:S(2)}) async-start(bf16[8,128,128]{2,1,0:T(8,128)(2,1)} %collective-permute-done.1), calls=%async_computation.1 | async-start | bytes 524288 | tf_op jit(solution)/shard_map/all_to_all | solution.py:254
  51.7 1.9 %collective-permute-start.2 = (bf16[7,128,128]{2,1,0:T(8,128)(2,1)S(1)}, bf16[7,128,128]{2,1,0:T(8,128)(2,1)S(1)}, u32[]{:S(2)}, u32[]{:S(2)}) collective-permute-start(bf16[7,128,128]{2,1,0:T(8,128)(2,1)S(1)} %get-tuple-element.37), channel_id=1, source_target_pairs={{0,24},{2,26},{4,28},{6,30},{8,16},{10,18},{12,20},{14,22},{16,40}... | collective-permute-start | bytes 688136 | tf_op jit(solution)/shard_map/ppermute | solution.py:248
  53.7 1.9 %collective-permute-start = (bf16[7,128,128]{2,1,0:T(8,128)(2,1)S(1)}, bf16[7,128,128]{2,1,0:T(8,128)(2,1)S(1)}, u32[]{:S(2)}, u32[]{:S(2)}) collective-permute-start(bf16[7,128,128]{2,1,0:T(8,128)(2,1)S(1)} %get-tuple-element.38), channel_id=1, source_target_pairs={{0,24},{2,26},{4,28},{6,30},{8,16},{10,18},{12,20},{14,22},{16,40}... | collective-permute-start | bytes 688136 | tf_op jit(solution)/shard_map/ppermute | solution.py:248
  56.2 0.1 pad_add_fusion.refs_0_
  56.3 2.6 %all-to-all-done.1.refs_1_ = bf16[8,128,128]{2,1,0:T(8,128)(2,1)S(1)} async-done(((bf16[8,128,128]{2,1,0:T(8,128)(2,1)}), bf16[8,128,128]{2,1,0:T(8,128)(2,1)S(1)}, u32[]{:S(2)}, u32[]{:S(2)}) %all-to-all-start.1) | async-done | bytes 262176 | tf_op jit(solution)/shard_map/all_to_all | solution.py:254
  58.9 3.2 %collective-permute-done.2.refs_3_ = bf16[7,128,128]{2,1,0:T(8,128)(2,1)S(1)} collective-permute-done((bf16[7,128,128]{2,1,0:T(8,128)(2,1)S(1)}, bf16[7,128,128]{2,1,0:T(8,128)(2,1)S(1)}, u32[]{:S(2)}, u32[]{:S(2)}) %collective-permute-start.2) | collective-permute-done | bytes 229408 | tf_op jit(solution)/shard_map/ppermute | solution.py:248
  62.2 4.8 %attention_cross.1 = (bf16[8,128,128]{2,1,0:T(8,128)(2,1)S(1)}, f32[8,128,128]{2,1,0:T(8,128)S(1)}, bf16[7,128,128]{2,1,0:T(8,128)(2,1)S(1)}) custom-call(s32[2]{0:T(128)S(1)} %pad_add_fusion.refs_0_, bf16[8,128,128]{2,1,0:T(8,128)(2,1)S(1)} %all-to-all-done.1.refs_1_, bf16[8,3,128,128]{3,2,1,0:T(8,128)(2,1)S(1)} %all-to-all-done.refs_1_.refs_2_, ...), custom_call_target="tpu_custom_call" | custom-call | tf_op jit(solution)/shard_map/attention_cross/pallas_call | solution.py:182
  67.0 12.1 %collective-permute-start.5 = (bf16[8,128,128]{2,1,0:T(8,128)(2,1)S(1)}, bf16[8,128,128]{2,1,0:T(8,128)(2,1)S(1)}, u32[]{:S(2)}, u32[]{:S(2)}) collective-permute-start(bf16[8,128,128]{2,1,0:T(8,128)(2,1)S(1)} %get-tuple-element.28), channel_id=1, source_target_pairs={{0,256},{256,0},{1,257},{257,1},{2,258},{258,2},{3,259},{259,3},{4... | collective-permute-start | bytes 786440 | tf_op jit(solution)/shard_map/ppermute | solution.py:258
  79.1 4.1 %collective-permute-start.4 = (bf16[7,128,128]{2,1,0:T(8,128)(2,1)S(1)}, bf16[7,128,128]{2,1,0:T(8,128)(2,1)S(1)}, u32[]{:S(2)}, u32[]{:S(2)}) collective-permute-start(bf16[7,128,128]{2,1,0:T(8,128)(2,1)S(1)} %get-tuple-element.27), channel_id=1, source_target_pairs={{0,248},{2,250},{4,252},{6,254},{8,240},{10,242},{12,244},{14,246}... | collective-permute-start | bytes 688136 | tf_op jit(solution)/shard_map/ppermute | solution.py:248
  83.2 5.5 %attention_self.1 = (bf16[8,128,128]{2,1,0:T(8,128)(2,1)}, f32[8,128,128]{2,1,0:T(8,128)S(1)}, bf16[7,128,128]{2,1,0:T(8,128)(2,1)S(1)}) custom-call(s32[2]{0:T(128)S(1)} %pad_add_fusion.refs_0_, bf16[8,3,128,128]{3,2,1,0:T(8,128)(2,1)S(1)} %all-to-all-done.refs_1_.refs_2_, bf16[7,128,128]{2,1,0:T(8,128)(2,1)S(1)} %collective-permute-done.refs_2_), custom_call_target="tpu_custom_call" | custom-call | tf_op jit(solution)/shard_map/attention_self/pallas_call | solution.py:182
  88.7 1.9 %collective-permute-start.3 = (bf16[7,128,128]{2,1,0:T(8,128)(2,1)S(1)}, bf16[7,128,128]{2,1,0:T(8,128)(2,1)S(1)}, u32[]{:S(2)}, u32[]{:S(2)}) collective-permute-start(bf16[7,128,128]{2,1,0:T(8,128)(2,1)S(1)} %get-tuple-element.26), channel_id=1, source_target_pairs={{0,248},{2,250},{4,252},{6,254},{8,240},{10,242},{12,244},{14,246}... | collective-permute-start | bytes 688136 | tf_op jit(solution)/shard_map/ppermute | solution.py:248
  90.6 5.1 %all-to-all-start.3 = ((bf16[8,128,128]{2,1,0:T(8,128)(2,1)}), bf16[8,128,128]{2,1,0:T(8,128)(2,1)S(1)}, u32[]{:S(2)}, u32[]{:S(2)}) async-start(bf16[8,128,128]{2,1,0:T(8,128)(2,1)} %get-tuple-element.29), calls=%async_computation.3 | async-start | bytes 524288 | tf_op jit(solution)/shard_map/all_to_all | solution.py:254
  95.6 5.5 %collective-permute-done.4.home_c = bf16[7,128,128]{2,1,0:T(8,128)(2,1)S(1)} collective-permute-done((bf16[7,128,128]{2,1,0:T(8,128)(2,1)S(1)}, bf16[7,128,128]{2,1,0:T(8,128)(2,1)S(1)}, u32[]{:S(2)}, u32[]{:S(2)}) %collective-permute-start.4) | collective-permute-done | bytes 229408 | tf_op jit(solution)/shard_map/ppermute | solution.py:248
  101.2 4.8 %collective-permute-done.3.home_s = bf16[7,128,128]{2,1,0:T(8,128)(2,1)S(1)} collective-permute-done((bf16[7,128,128]{2,1,0:T(8,128)(2,1)S(1)}, bf16[7,128,128]{2,1,0:T(8,128)(2,1)S(1)}, u32[]{:S(2)}, u32[]{:S(2)}) %collective-permute-start.3) | collective-permute-done | bytes 229408 | tf_op jit(solution)/shard_map/ppermute | solution.py:248
  106.0 0.0 collective-permute-done.5.out_c
  106.0 0.1 join.1
  106.1 0.0 all-to-all-done.3.parts_s
  106.1 19.3 %all_to_all.20.parts = bf16[8,3,128,128]{3,2,1,0:T(8,128)(2,1)S(1)} all-to-all(bf16[8,3,128,128]{3,2,1,0:T(8,128)(2,1)S(1)} %join.1), channel_id=1, replica_groups={{0,2,4,6,8,10,12,14},{16,18,20,22,24,26,28,30},{32,34,36,38,40,42,44,46..., dimensions={0} | all-to-all | bytes 1572864 | tf_op jit(solution)/shard_map/all_to_all | solution.py:254
  125.4 1.2 unpack.1
  (2 shorter events, 0.0 us)
Async XLA Ops:
  3.1 43.1 %all-to-all-start = ((bf16[8,3,128,128]{3,2,1,0:T(8,128)(2,1)}), bf16[8,3,128,128]{3,2,1,0:T(8,128)(2,1)S(1)}, u32[]{:S(2)}, u32[]{:S(2)}) async-start(bf16[8,3,128,128]{3,2,1,0:T(8,128)(2,1)} %get-tuple-element.22), calls=%async_computation | async-start | bytes 1572864 | tf_op jit(solution)/shard_map/all_to_all | solution.py:254
  8.2 38.0 %collective-permute-start.1 = (bf16[8,128,128]{2,1,0:T(8,128)(2,1)S(1)}, bf16[8,128,128]{2,1,0:T(8,128)(2,1)}, u32[]{:S(2)}, u32[]{:S(2)}) collective-permute-start(bf16[8,128,128]{2,1,0:T(8,128)(2,1)S(1)} %get-tuple-element.24), channel_id=1, source_target_pairs={{0,256},{256,0},{1,257},{257,1},{2,258},{258,2},{3,259},{259,3},{4... | collective-permute-start | bytes 786440 | tf_op jit(solution)/shard_map/ppermute | solution.py:258
  46.3 12.7 %all-to-all-start.1 = ((bf16[8,128,128]{2,1,0:T(8,128)(2,1)}), bf16[8,128,128]{2,1,0:T(8,128)(2,1)S(1)}, u32[]{:S(2)}, u32[]{:S(2)}) async-start(bf16[8,128,128]{2,1,0:T(8,128)(2,1)} %collective-permute-done.1), calls=%async_computation.1 | async-start | bytes 524288 | tf_op jit(solution)/shard_map/all_to_all | solution.py:254
  51.7 10.4 %collective-permute-start.2 = (bf16[7,128,128]{2,1,0:T(8,128)(2,1)S(1)}, bf16[7,128,128]{2,1,0:T(8,128)(2,1)S(1)}, u32[]{:S(2)}, u32[]{:S(2)}) collective-permute-start(bf16[7,128,128]{2,1,0:T(8,128)(2,1)S(1)} %get-tuple-element.37), channel_id=1, source_target_pairs={{0,24},{2,26},{4,28},{6,30},{8,16},{10,18},{12,20},{14,22},{16,40}... | collective-permute-start | bytes 688136 | tf_op jit(solution)/shard_map/ppermute | solution.py:248
  53.7 29.5 %collective-permute-start = (bf16[7,128,128]{2,1,0:T(8,128)(2,1)S(1)}, bf16[7,128,128]{2,1,0:T(8,128)(2,1)S(1)}, u32[]{:S(2)}, u32[]{:S(2)}) collective-permute-start(bf16[7,128,128]{2,1,0:T(8,128)(2,1)S(1)} %get-tuple-element.38), channel_id=1, source_target_pairs={{0,24},{2,26},{4,28},{6,30},{8,16},{10,18},{12,20},{14,22},{16,40}... | collective-permute-start | bytes 688136 | tf_op jit(solution)/shard_map/ppermute | solution.py:248
  67.0 39.0 %collective-permute-start.5 = (bf16[8,128,128]{2,1,0:T(8,128)(2,1)S(1)}, bf16[8,128,128]{2,1,0:T(8,128)(2,1)S(1)}, u32[]{:S(2)}, u32[]{:S(2)}) collective-permute-start(bf16[8,128,128]{2,1,0:T(8,128)(2,1)S(1)} %get-tuple-element.28), channel_id=1, source_target_pairs={{0,256},{256,0},{1,257},{257,1},{2,258},{258,2},{3,259},{259,3},{4... | collective-permute-start | bytes 786440 | tf_op jit(solution)/shard_map/ppermute | solution.py:258
  79.1 22.1 %collective-permute-start.4 = (bf16[7,128,128]{2,1,0:T(8,128)(2,1)S(1)}, bf16[7,128,128]{2,1,0:T(8,128)(2,1)S(1)}, u32[]{:S(2)}, u32[]{:S(2)}) collective-permute-start(bf16[7,128,128]{2,1,0:T(8,128)(2,1)S(1)} %get-tuple-element.27), channel_id=1, source_target_pairs={{0,248},{2,250},{4,252},{6,254},{8,240},{10,242},{12,244},{14,246}... | collective-permute-start | bytes 688136 | tf_op jit(solution)/shard_map/ppermute | solution.py:248
  88.7 17.3 %collective-permute-start.3 = (bf16[7,128,128]{2,1,0:T(8,128)(2,1)S(1)}, bf16[7,128,128]{2,1,0:T(8,128)(2,1)S(1)}, u32[]{:S(2)}, u32[]{:S(2)}) collective-permute-start(bf16[7,128,128]{2,1,0:T(8,128)(2,1)S(1)} %get-tuple-element.26), channel_id=1, source_target_pairs={{0,248},{2,250},{4,252},{6,254},{8,240},{10,242},{12,244},{14,246}... | collective-permute-start | bytes 688136 | tf_op jit(solution)/shard_map/ppermute | solution.py:248
  90.6 15.5 %all-to-all-start.3 = ((bf16[8,128,128]{2,1,0:T(8,128)(2,1)}), bf16[8,128,128]{2,1,0:T(8,128)(2,1)S(1)}, u32[]{:S(2)}, u32[]{:S(2)}) async-start(bf16[8,128,128]{2,1,0:T(8,128)(2,1)} %get-tuple-element.29), calls=%async_computation.3 | async-start | bytes 524288 | tf_op jit(solution)/shard_map/all_to_all | solution.py:254

commit v5 on v4

--- a/solution.py
+++ b/solution.py
@@ -72,7 +72,7 @@
     else:
         qdo, own, halo, out, dkv_own, dkv_halo, kv_t, scores, probs, stacks = refs
         queries = [qdo.at[b] for b in range(TEAM)]
-    blocks = [halo.at[b] for b in range(HALO)] + [own.at[b, kind] for b in range(TEAM)]
+    blocks = [halo.at[b, kind] for b in range(HALO)] + [own.at[b, kind] for b in range(TEAM)]
     first_half = lax.broadcasted_iota(jnp.int32, (ROWS, PAIR), 1) < HEAD
     causal = lax.broadcasted_iota(jnp.int32, (ROWS, ROWS), 0) <= lax.broadcasted_iota(
         jnp.int32, (ROWS, ROWS), 1
@@ -276,11 +276,10 @@
     )
     arrived = swapped(far)
     own = within_team(near)
-    halo_c = to_next_team(own[1:, CROSS], 1)
-    halo_s = to_next_team(own[1:, SELF], 1)
+    halo = to_next_team(own[1:, :NEAR], 1)
     crossing = within_team(arrived)
-    out_s, own_s, back_s = attention(SELF, slots, own, halo_s)
-    out_c, own_c, back_c = attention(CROSS, slots, crossing, own, halo_c)
+    out_s, own_s, back_s = attention(SELF, slots, own, halo)
+    out_c, own_c, back_c = attention(CROSS, slots, crossing, own, halo)
     home_s = to_next_team(back_s, -1)
     home_c = to_next_team(back_c, -1)
     joined = local_call(

time: 127 us -> 123 us (0.969)
  the two profiles are of different devices: /device:TPU:36 before, /device:TPU:64 now
where the time goes in v5:
time: 123 us
  starting transfers between devices  54.3 us (44%)
  waiting for transfers between devices  31.4 us (26%)
  blocking collectives  21.5 us (17%)
  Pallas kernels  14.1 us (11%)
  between operations  1.39 us (1%)
    ppermute x2, starting transfers between devices, swapped(): return lax.ppermute(value, 'tower', [(0, 1), (1, 0)])  26.6 us
    all_to_all x1, blocking collectives, within_team(): lax.all_to_all(value, 'ctx', 0, 0, axis_index_groups=teams, tiled=True)  21.5 us
    ppermute x3, waiting for transfers between devices, to_next_team(): return lax.ppermute(value, 'ctx', route)  15 us
    all_to_all x3, starting transfers between devices, within_team(): lax.all_to_all(value, 'ctx', 0, 0, axis_index_groups=teams, tiled=True)  14.3 us
    ppermute x3, starting transfers between devices, to_next_team(): return lax.ppermute(value, 'ctx', route)  13.4 us
    pallas_call x2, Pallas kernels, attention(): pl.pallas_call(kernel, out_shape=(block_shape(TEAM), block_shape(TEAM, dt...  10.3 us
    ppermute x2, waiting for transfers between devices, swapped(): return lax.ppermute(value, 'tower', [(0, 1), (1, 0)])  9.98 us
    all_to_all x3, waiting for transfers between devices, within_team(): lax.all_to_all(value, 'ctx', 0, 0, axis_index_groups=teams, tiled=True)  6.49 us
  transfers between devices with their start and end apart: 8, of which 5 were waited for; matrix products, arithmetic and copies ran while one was open for 0% of the time, Pallas kernels for 5%

profile of v5, /device:TPU:64, one launch (start us, length us, event | category | flops | bytes accessed | tf_op | source)
XLA Modules:
  0.0 122.8 jit_solution(7798320793233482914)
XLA Ops:
  0.6 2.5 %pack.1 = (bf16[8,128,128]{2,1,0:T(8,128)(2,1)S(1)}, bf16[8,3,128,128]{3,2,1,0:T(8,128)(2,1)}) custom-call(bf16[128,512]{1,0:T(8,128)(2,1)} %bitcast.17, bf16[128,512]{1,0:T(8,128)(2,1)} %bitcast.18, bf16[128,512]{1,0:T(8,128)(2,1)} %bitcast.19, bf16[128,512]{1,0:T(8,128)(2,1)} %bitcast.20, bf16[128,512]{1,0:T(8,128)(2,1)} %bitcast.21, ...), custom_call_target="tpu_custom_call" | custom-call | tf_op jit(solution)/shard_map/pack/pallas_call | solution.py:233
  3.1 5.4 %all-to-all-start = ((bf16[8,3,128,128]{3,2,1,0:T(8,128)(2,1)}), bf16[8,3,128,128]{3,2,1,0:T(8,128)(2,1)S(1)}, u32[]{:S(2)}, u32[]{:S(2)}) async-start(bf16[8,3,128,128]{3,2,1,0:T(8,128)(2,1)} %get-tuple-element.22), calls=%async_computation | async-start | bytes 1572864 | tf_op jit(solution)/shard_map/all_to_all | solution.py:254
  8.5 13.9 %collective-permute-start.1 = (bf16[8,128,128]{2,1,0:T(8,128)(2,1)S(1)}, bf16[8,128,128]{2,1,0:T(8,128)(2,1)}, u32[]{:S(2)}, u32[]{:S(2)}) collective-permute-start(bf16[8,128,128]{2,1,0:T(8,128)(2,1)S(1)} %get-tuple-element.24), channel_id=1, source_target_pairs={{0,256},{256,0},{1,257},{257,1},{2,258},{258,2},{3,259},{259,3},{4... | collective-permute-start | bytes 786440 | tf_op jit(solution)/shard_map/ppermute | solution.py:258
  22.5 0.0 all-to-all-done.refs_1_.refs_2_
  22.5 5.2 %collective-permute-start = (bf16[7,2,128,128]{3,2,1,0:T(8,128)(2,1)S(1)}, bf16[7,2,128,128]{3,2,1,0:T(8,128)(2,1)S(1)}, u32[]{:S(2)}, u32[]{:S(2)}) collective-permute-start(bf16[7,2,128,128]{3,2,1,0:T(8,128)(2,1)S(1)} %slice.4), channel_id=1, source_target_pairs={{0,24},{2,26},{4,28},{6,30},{8,16},{10,18},{12,20},{14,22},{16,40}... | collective-permute-start | bytes 1376264 | tf_op jit(solution)/shard_map/ppermute | solution.py:248
  27.7 10.0 %collective-permute-done.1 = bf16[8,128,128]{2,1,0:T(8,128)(2,1)} collective-permute-done((bf16[8,128,128]{2,1,0:T(8,128)(2,1)S(1)}, bf16[8,128,128]{2,1,0:T(8,128)(2,1)}, u32[]{:S(2)}, u32[]{:S(2)}) %collective-permute-start.1) | collective-permute-done | bytes 262176 | tf_op jit(solution)/shard_map/ppermute | solution.py:258
  37.7 5.4 %all-to-all-start.1 = ((bf16[8,128,128]{2,1,0:T(8,128)(2,1)}), bf16[8,128,128]{2,1,0:T(8,128)(2,1)S(1)}, u32[]{:S(2)}, u32[]{:S(2)}) async-start(bf16[8,128,128]{2,1,0:T(8,128)(2,1)} %collective-permute-done.1), calls=%async_computation.1 | async-start | bytes 524288 | tf_op jit(solution)/shard_map/all_to_all | solution.py:254
  43.8 0.1 pad_add_fusion.refs_0_
  43.9 6.5 %all-to-all-done.1.refs_1_ = bf16[8,128,128]{2,1,0:T(8,128)(2,1)S(1)} async-done(((bf16[8,128,128]{2,1,0:T(8,128)(2,1)}), bf16[8,128,128]{2,1,0:T(8,128)(2,1)S(1)}, u32[]{:S(2)}, u32[]{:S(2)}) %all-to-all-start.1) | async-done | bytes 262176 | tf_op jit(solution)/shard_map/all_to_all | solution.py:254
  50.3 6.7 %collective-permute-done.refs_2_.refs_3_ = bf16[7,2,128,128]{3,2,1,0:T(8,128)(2,1)S(1)} collective-permute-done((bf16[7,2,128,128]{3,2,1,0:T(8,128)(2,1)S(1)}, bf16[7,2,128,128]{3,2,1,0:T(8,128)(2,1)S(1)}, u32[]{:S(2)}, u32[]{:S(2)}) %collective-permute-start) | collective-permute-done | bytes 458784 | tf_op jit(solution)/shard_map/ppermute | solution.py:248
  57.0 4.8 %attention_cross.1 = (bf16[8,128,128]{2,1,0:T(8,128)(2,1)S(1)}, f32[8,128,128]{2,1,0:T(8,128)S(1)}, bf16[7,128,128]{2,1,0:T(8,128)(2,1)S(1)}) custom-call(s32[2]{0:T(128)S(1)} %pad_add_fusion.refs_0_, bf16[8,128,128]{2,1,0:T(8,128)(2,1)S(1)} %all-to-all-done.1.refs_1_, bf16[8,3,128,128]{3,2,1,0:T(8,128)(2,1)S(1)} %all-to-all-done.refs_1_.refs_2_, ...), custom_call_target="tpu_custom_call" | custom-call | tf_op jit(solution)/shard_map/attention_cross/pallas_call | solution.py:182
  61.8 12.7 %collective-permute-start.4 = (bf16[8,128,128]{2,1,0:T(8,128)(2,1)S(1)}, bf16[8,128,128]{2,1,0:T(8,128)(2,1)S(1)}, u32[]{:S(2)}, u32[]{:S(2)}) collective-permute-start(bf16[8,128,128]{2,1,0:T(8,128)(2,1)S(1)} %get-tuple-element.28), channel_id=1, source_target_pairs={{0,256},{256,0},{1,257},{257,1},{2,258},{258,2},{3,259},{259,3},{4... | collective-permute-start | bytes 786440 | tf_op jit(solution)/shard_map/ppermute | solution.py:258
  74.6 5.8 %collective-permute-start.3 = (bf16[7,128,128]{2,1,0:T(8,128)(2,1)S(1)}, bf16[7,128,128]{2,1,0:T(8,128)(2,1)S(1)}, u32[]{:S(2)}, u32[]{:S(2)}) collective-permute-start(bf16[7,128,128]{2,1,0:T(8,128)(2,1)S(1)} %get-tuple-element.27), channel_id=1, source_target_pairs={{0,248},{2,250},{4,252},{6,254},{8,240},{10,242},{12,244},{14,246}... | collective-permute-start | bytes 688136 | tf_op jit(solution)/shard_map/ppermute | solution.py:248
  80.3 5.5 %attention_self.1 = (bf16[8,128,128]{2,1,0:T(8,128)(2,1)}, f32[8,128,128]{2,1,0:T(8,128)S(1)}, bf16[7,128,128]{2,1,0:T(8,128)(2,1)}) custom-call(s32[2]{0:T(128)S(1)} %pad_add_fusion.refs_0_, bf16[8,3,128,128]{3,2,1,0:T(8,128)(2,1)S(1)} %all-to-all-done.refs_1_.refs_2_, bf16[7,2,128,128]{3,2,1,0:T(8,128)(2,1)S(1)} %collective-permute-done.refs_2_.refs_3_), custom_call_target="tpu_custom_call" | custom-call | tf_op jit(solution)/shard_map/attention_self/pallas_call | solution.py:182
  85.8 2.5 %collective-permute-start.2 = (bf16[7,128,128]{2,1,0:T(8,128)(2,1)}, bf16[7,128,128]{2,1,0:T(8,128)(2,1)S(1)}, u32[]{:S(2)}, u32[]{:S(2)}) collective-permute-start(bf16[7,128,128]{2,1,0:T(8,128)(2,1)} %get-tuple-element.26), channel_id=1, source_target_pairs={{0,248},{2,250},{4,252},{6,254},{8,240},{10,242},{12,244},{14,246}... | collective-permute-start | bytes 688136 | tf_op jit(solution)/shard_map/ppermute | solution.py:248
  88.3 3.4 %all-to-all-start.3 = ((bf16[8,128,128]{2,1,0:T(8,128)(2,1)}), bf16[8,128,128]{2,1,0:T(8,128)(2,1)S(1)}, u32[]{:S(2)}, u32[]{:S(2)}) async-start(bf16[8,128,128]{2,1,0:T(8,128)(2,1)} %get-tuple-element.29), calls=%async_computation.3 | async-start | bytes 524288 | tf_op jit(solution)/shard_map/all_to_all | solution.py:254
  91.7 3.7 %collective-permute-done.3.home_c = bf16[7,128,128]{2,1,0:T(8,128)(2,1)S(1)} collective-permute-done((bf16[7,128,128]{2,1,0:T(8,128)(2,1)S(1)}, bf16[7,128,128]{2,1,0:T(8,128)(2,1)S(1)}, u32[]{:S(2)}, u32[]{:S(2)}) %collective-permute-start.3) | collective-permute-done | bytes 229408 | tf_op jit(solution)/shard_map/ppermute | solution.py:248
  95.4 4.6 %collective-permute-done.2.home_s = bf16[7,128,128]{2,1,0:T(8,128)(2,1)S(1)} collective-permute-done((bf16[7,128,128]{2,1,0:T(8,128)(2,1)}, bf16[7,128,128]{2,1,0:T(8,128)(2,1)S(1)}, u32[]{:S(2)}, u32[]{:S(2)}) %collective-permute-start.2) | collective-permute-done | bytes 229408 | tf_op jit(solution)/shard_map/ppermute | solution.py:248
  100.0 0.0 collective-permute-done.4.out_c
  100.0 0.1 join.1
  100.1 0.0 all-to-all-done.3.parts_s
  100.1 21.5 %all_to_all.20.parts = bf16[8,3,128,128]{3,2,1,0:T(8,128)(2,1)S(1)} all-to-all(bf16[8,3,128,128]{3,2,1,0:T(8,128)(2,1)S(1)} %join.1), channel_id=1, replica_groups={{0,2,4,6,8,10,12,14},{16,18,20,22,24,26,28,30},{32,34,36,38,40,42,44,46..., dimensions={0} | all-to-all | bytes 1572864 | tf_op jit(solution)/shard_map/all_to_all | solution.py:254
  121.6 1.2 unpack.1
  (1 shorter events, 0.0 us)
Async XLA Ops:
  3.1 19.3 %all-to-all-start = ((bf16[8,3,128,128]{3,2,1,0:T(8,128)(2,1)}), bf16[8,3,128,128]{3,2,1,0:T(8,128)(2,1)S(1)}, u32[]{:S(2)}, u32[]{:S(2)}) async-start(bf16[8,3,128,128]{3,2,1,0:T(8,128)(2,1)} %get-tuple-element.22), calls=%async_computation | async-start | bytes 1572864 | tf_op jit(solution)/shard_map/all_to_all | solution.py:254
  8.5 29.2 %collective-permute-start.1 = (bf16[8,128,128]{2,1,0:T(8,128)(2,1)S(1)}, bf16[8,128,128]{2,1,0:T(8,128)(2,1)}, u32[]{:S(2)}, u32[]{:S(2)}) collective-permute-start(bf16[8,128,128]{2,1,0:T(8,128)(2,1)S(1)} %get-tuple-element.24), channel_id=1, source_target_pairs={{0,256},{256,0},{1,257},{257,1},{2,258},{258,2},{3,259},{259,3},{4... | collective-permute-start | bytes 786440 | tf_op jit(solution)/shard_map/ppermute | solution.py:258
  22.5 34.5 %collective-permute-start = (bf16[7,2,128,128]{3,2,1,0:T(8,128)(2,1)S(1)}, bf16[7,2,128,128]{3,2,1,0:T(8,128)(2,1)S(1)}, u32[]{:S(2)}, u32[]{:S(2)}) collective-permute-start(bf16[7,2,128,128]{3,2,1,0:T(8,128)(2,1)S(1)} %slice.4), channel_id=1, source_target_pairs={{0,24},{2,26},{4,28},{6,30},{8,16},{10,18},{12,20},{14,22},{16,40}... | collective-permute-start | bytes 1376264 | tf_op jit(solution)/shard_map/ppermute | solution.py:248
  37.7 12.6 %all-to-all-start.1 = ((bf16[8,128,128]{2,1,0:T(8,128)(2,1)}), bf16[8,128,128]{2,1,0:T(8,128)(2,1)S(1)}, u32[]{:S(2)}, u32[]{:S(2)}) async-start(bf16[8,128,128]{2,1,0:T(8,128)(2,1)} %collective-permute-done.1), calls=%async_computation.1 | async-start | bytes 524288 | tf_op jit(solution)/shard_map/all_to_all | solution.py:254
  61.8 38.2 %collective-permute-start.4 = (bf16[8,128,128]{2,1,0:T(8,128)(2,1)S(1)}, bf16[8,128,128]{2,1,0:T(8,128)(2,1)S(1)}, u32[]{:S(2)}, u32[]{:S(2)}) collective-permute-start(bf16[8,128,128]{2,1,0:T(8,128)(2,1)S(1)} %get-tuple-element.28), channel_id=1, source_target_pairs={{0,256},{256,0},{1,257},{257,1},{2,258},{258,2},{3,259},{259,3},{4... | collective-permute-start | bytes 786440 | tf_op jit(solution)/shard_map/ppermute | solution.py:258
  74.6 20.9 %collective-permute-start.3 = (bf16[7,128,128]{2,1,0:T(8,128)(2,1)S(1)}, bf16[7,128,128]{2,1,0:T(8,128)(2,1)S(1)}, u32[]{:S(2)}, u32[]{:S(2)}) collective-permute-start(bf16[7,128,128]{2,1,0:T(8,128)(2,1)S(1)} %get-tuple-element.27), channel_id=1, source_target_pairs={{0,248},{2,250},{4,252},{6,254},{8,240},{10,242},{12,244},{14,246}... | collective-permute-start | bytes 688136 | tf_op jit(solution)/shard_map/ppermute | solution.py:248
  85.8 14.2 %collective-permute-start.2 = (bf16[7,128,128]{2,1,0:T(8,128)(2,1)}, bf16[7,128,128]{2,1,0:T(8,128)(2,1)S(1)}, u32[]{:S(2)}, u32[]{:S(2)}) collective-permute-start(bf16[7,128,128]{2,1,0:T(8,128)(2,1)} %get-tuple-element.26), channel_id=1, source_target_pairs={{0,248},{2,250},{4,252},{6,254},{8,240},{10,242},{12,244},{14,246}... | collective-permute-start | bytes 688136 | tf_op jit(solution)/shard_map/ppermute | solution.py:248
  88.3 11.8 %all-to-all-start.3 = ((bf16[8,128,128]{2,1,0:T(8,128)(2,1)}), bf16[8,128,128]{2,1,0:T(8,128)(2,1)S(1)}, u32[]{:S(2)}, u32[]{:S(2)}) async-start(bf16[8,128,128]{2,1,0:T(8,128)(2,1)} %get-tuple-element.29), calls=%async_computation.3 | async-start | bytes 524288 | tf_op jit(solution)/shard_map/all_to_all | solution.py:254

commit v6 on v4

--- a/solution.py
+++ b/solution.py
@@ -278,6 +278,7 @@
     own = within_team(near)
     halo_c = to_next_team(own[1:, CROSS], 1)
     halo_s = to_next_team(own[1:, SELF], 1)
+    arrived, halo_c = lax.optimization_barrier((arrived, halo_c))
     crossing = within_team(arrived)
     out_s, own_s, back_s = attention(SELF, slots, own, halo_s)
     out_c, own_c, back_c = attention(CROSS, slots, crossing, own, halo_c)

time: 127 us -> 127 us (level)
  the two profiles are of different devices: /device:TPU:36 before, /device:TPU:128 now
where the time goes in v6:
time: 127 us; the launch traced here: 126 us
  waiting for transfers between devices  50.3 us (40%)
  starting transfers between devices  47.3 us (37%)
  Pallas kernels  14.1 us (11%)
  blocking collectives  12.9 us (10%)
  between operations  1.39 us (1%)
    ppermute x2, waiting for transfers between devices, swapped(): return lax.ppermute(value, 'tower', [(0, 1), (1, 0)])  27.5 us
    ppermute x4, starting transfers between devices, to_next_team(): return lax.ppermute(value, 'ctx', route)  20.6 us
    ppermute x4, waiting for transfers between devices, to_next_team(): return lax.ppermute(value, 'ctx', route)  17 us
    all_to_all x3, starting transfers between devices, within_team(): lax.all_to_all(value, 'ctx', 0, 0, axis_index_groups=teams, tiled=True)  13.9 us
    all_to_all x1, blocking collectives, within_team(): lax.all_to_all(value, 'ctx', 0, 0, axis_index_groups=teams, tiled=True)  12.9 us
    ppermute x2, starting transfers between devices, swapped(): return lax.ppermute(value, 'tower', [(0, 1), (1, 0)])  12.8 us
    pallas_call x2, Pallas kernels, attention(): pl.pallas_call(kernel, out_shape=(block_shape(TEAM), block_shape(TEAM, dt...  10.3 us
    all_to_all x3, waiting for transfers between devices, within_team(): lax.all_to_all(value, 'ctx', 0, 0, axis_index_groups=teams, tiled=True)  5.8 us
  transfers between devices with their start and end apart: 9, of which 7 were waited for; matrix products, arithmetic and copies ran while one was open for 0% of the time, Pallas kernels for 8%

profile of v6, /device:TPU:128, one launch (start us, length us, event | category | flops | bytes accessed | tf_op | source)
XLA Modules:
  0.0 126.1 jit_solution(17992895780519182456)
XLA Ops:
  0.6 2.5 %pack.1 = (bf16[8,128,128]{2,1,0:T(8,128)(2,1)S(1)}, bf16[8,3,128,128]{3,2,1,0:T(8,128)(2,1)}) custom-call(bf16[128,512]{1,0:T(8,128)(2,1)} %bitcast.25, bf16[128,512]{1,0:T(8,128)(2,1)} %bitcast.26, bf16[128,512]{1,0:T(8,128)(2,1)} %bitcast.27, bf16[128,512]{1,0:T(8,128)(2,1)} %bitcast.28, bf16[128,512]{1,0:T(8,128)(2,1)} %bitcast.29, ...), custom_call_target="tpu_custom_call" | custom-call | tf_op jit(solution)/shard_map/pack/pallas_call | solution.py:233
  3.1 5.4 %all-to-all-start = ((bf16[8,3,128,128]{3,2,1,0:T(8,128)(2,1)}), bf16[8,3,128,128]{3,2,1,0:T(8,128)(2,1)S(1)}, u32[]{:S(2)}, u32[]{:S(2)}) async-start(bf16[8,3,128,128]{3,2,1,0:T(8,128)(2,1)} %get-tuple-element.24), calls=%async_computation | async-start | bytes 1572864 | tf_op jit(solution)/shard_map/all_to_all | solution.py:254
  8.5 10.9 %collective-permute-start.1 = (bf16[8,128,128]{2,1,0:T(8,128)(2,1)S(1)}, bf16[8,128,128]{2,1,0:T(8,128)(2,1)}, u32[]{:S(2)}, u32[]{:S(2)}) collective-permute-start(bf16[8,128,128]{2,1,0:T(8,128)(2,1)S(1)} %get-tuple-element.26), channel_id=1, source_target_pairs={{0,256},{256,0},{1,257},{257,1},{2,258},{258,2},{3,259},{259,3},{4... | collective-permute-start | bytes 786440 | tf_op jit(solution)/shard_map/ppermute | solution.py:258
  19.4 1.1 all-to-all-done.refs_1_.refs_2_
  20.6 4.6 %collective-permute-start.2 = (bf16[7,128,128]{2,1,0:T(8,128)(2,1)S(1)}, bf16[7,128,128]{2,1,0:T(8,128)(2,1)S(1)}, u32[]{:S(2)}, u32[]{:S(2)}) collective-permute-start(bf16[7,128,128]{2,1,0:T(8,128)(2,1)S(1)} %get-tuple-element.41), channel_id=1, source_target_pairs={{0,24},{2,26},{4,28},{6,30},{8,16},{10,18},{12,20},{14,22},{16,40}... | collective-permute-start | bytes 688136 | tf_op jit(solution)/shard_map/ppermute | solution.py:248
  25.2 15.6 %collective-permute-done.1 = bf16[8,128,128]{2,1,0:T(8,128)(2,1)} collective-permute-done((bf16[8,128,128]{2,1,0:T(8,128)(2,1)S(1)}, bf16[8,128,128]{2,1,0:T(8,128)(2,1)}, u32[]{:S(2)}, u32[]{:S(2)}) %collective-permute-start.1) | collective-permute-done | bytes 262176 | tf_op jit(solution)/shard_map/ppermute | solution.py:258
  40.8 10.5 %collective-permute-done.2.refs_3_ = bf16[7,128,128]{2,1,0:T(8,128)(2,1)S(1)} collective-permute-done((bf16[7,128,128]{2,1,0:T(8,128)(2,1)S(1)}, bf16[7,128,128]{2,1,0:T(8,128)(2,1)S(1)}, u32[]{:S(2)}, u32[]{:S(2)}) %collective-permute-start.2) | collective-permute-done | bytes 229408 | tf_op jit(solution)/shard_map/ppermute | solution.py:248
  51.3 4.2 %all-to-all-start.1 = ((bf16[8,128,128]{2,1,0:T(8,128)(2,1)}), bf16[8,128,128]{2,1,0:T(8,128)(2,1)S(1)}, u32[]{:S(2)}, u32[]{:S(2)}) async-start(bf16[8,128,128]{2,1,0:T(8,128)(2,1)} %collective-permute-done.1), calls=%async_computation.1 | async-start | bytes 524288 | tf_op jit(solution)/shard_map/all_to_all | solution.py:254
  55.5 1.9 %collective-permute-start = (bf16[7,128,128]{2,1,0:T(8,128)(2,1)S(1)}, bf16[7,128,128]{2,1,0:T(8,128)(2,1)S(1)}, u32[]{:S(2)}, u32[]{:S(2)}) collective-permute-start(bf16[7,128,128]{2,1,0:T(8,128)(2,1)S(1)} %get-tuple-element.42), channel_id=1, source_target_pairs={{0,24},{2,26},{4,28},{6,30},{8,16},{10,18},{12,20},{14,22},{16,40}... | collective-permute-start | bytes 688136 | tf_op jit(solution)/shard_map/ppermute | solution.py:248
  58.1 0.1 pad_add_fusion.refs_0_
  58.2 4.7 %all-to-all-done.1.refs_1_ = bf16[8,128,128]{2,1,0:T(8,128)(2,1)S(1)} async-done(((bf16[8,128,128]{2,1,0:T(8,128)(2,1)}), bf16[8,128,128]{2,1,0:T(8,128)(2,1)S(1)}, u32[]{:S(2)}, u32[]{:S(2)}) %all-to-all-start.1) | async-done | bytes 262176 | tf_op jit(solution)/shard_map/all_to_all | solution.py:254
  62.9 4.8 %attention_cross.1 = (bf16[8,128,128]{2,1,0:T(8,128)(2,1)S(1)}, f32[8,128,128]{2,1,0:T(8,128)S(1)}, bf16[7,128,128]{2,1,0:T(8,128)(2,1)S(1)}) custom-call(s32[2]{0:T(128)S(1)} %pad_add_fusion.refs_0_, bf16[8,128,128]{2,1,0:T(8,128)(2,1)S(1)} %all-to-all-done.1.refs_1_, bf16[8,3,128,128]{3,2,1,0:T(8,128)(2,1)S(1)} %all-to-all-done.refs_1_.refs_2_, ...), custom_call_target="tpu_custom_call" | custom-call | tf_op jit(solution)/shard_map/attention_cross/pallas_call | solution.py:182
  67.8 1.9 %collective-permute-start.5 = (bf16[8,128,128]{2,1,0:T(8,128)(2,1)S(1)}, bf16[8,128,128]{2,1,0:T(8,128)(2,1)S(1)}, u32[]{:S(2)}, u32[]{:S(2)}) collective-permute-start(bf16[8,128,128]{2,1,0:T(8,128)(2,1)S(1)} %get-tuple-element.32), channel_id=1, source_target_pairs={{0,256},{256,0},{1,257},{257,1},{2,258},{258,2},{3,259},{259,3},{4... | collective-permute-start | bytes 786440 | tf_op jit(solution)/shard_map/ppermute | solution.py:258
  69.7 5.5 %attention_self.1 = (bf16[8,128,128]{2,1,0:T(8,128)(2,1)}, f32[8,128,128]{2,1,0:T(8,128)S(1)}, bf16[7,128,128]{2,1,0:T(8,128)(2,1)S(1)}) custom-call(s32[2]{0:T(128)S(1)} %pad_add_fusion.refs_0_, bf16[8,3,128,128]{3,2,1,0:T(8,128)(2,1)S(1)} %all-to-all-done.refs_1_.refs_2_, bf16[7,128,128]{2,1,0:T(8,128)(2,1)S(1)} %collective-permute-done.refs_2_), custom_call_target="tpu_custom_call" | custom-call | tf_op jit(solution)/shard_map/attention_self/pallas_call | solution.py:182
  75.1 12.1 %collective-permute-start.3 = (bf16[7,128,128]{2,1,0:T(8,128)(2,1)S(1)}, bf16[7,128,128]{2,1,0:T(8,128)(2,1)S(1)}, u32[]{:S(2)}, u32[]{:S(2)}) collective-permute-start(bf16[7,128,128]{2,1,0:T(8,128)(2,1)S(1)} %get-tuple-element.30), channel_id=1, source_target_pairs={{0,248},{2,250},{4,252},{6,254},{8,240},{10,242},{12,244},{14,246}... | collective-permute-start | bytes 688136 | tf_op jit(solution)/shard_map/ppermute | solution.py:248
  87.2 2.0 %collective-permute-start.4 = (bf16[7,128,128]{2,1,0:T(8,128)(2,1)S(1)}, bf16[7,128,128]{2,1,0:T(8,128)(2,1)S(1)}, u32[]{:S(2)}, u32[]{:S(2)}) collective-permute-start(bf16[7,128,128]{2,1,0:T(8,128)(2,1)S(1)} %get-tuple-element.31), channel_id=1, source_target_pairs={{0,248},{2,250},{4,252},{6,254},{8,240},{10,242},{12,244},{14,246}... | collective-permute-start | bytes 688136 | tf_op jit(solution)/shard_map/ppermute | solution.py:248
  89.2 4.2 %all-to-all-start.3 = ((bf16[8,128,128]{2,1,0:T(8,128)(2,1)}), bf16[8,128,128]{2,1,0:T(8,128)(2,1)S(1)}, u32[]{:S(2)}, u32[]{:S(2)}) async-start(bf16[8,128,128]{2,1,0:T(8,128)(2,1)} %get-tuple-element.33), calls=%async_computation.3 | async-start | bytes 524288 | tf_op jit(solution)/shard_map/all_to_all | solution.py:254
  93.4 3.8 %collective-permute-done.3.home_s = bf16[7,128,128]{2,1,0:T(8,128)(2,1)S(1)} collective-permute-done((bf16[7,128,128]{2,1,0:T(8,128)(2,1)S(1)}, bf16[7,128,128]{2,1,0:T(8,128)(2,1)S(1)}, u32[]{:S(2)}, u32[]{:S(2)}) %collective-permute-start.3) | collective-permute-done | bytes 229408 | tf_op jit(solution)/shard_map/ppermute | solution.py:248
  97.2 2.7 %collective-permute-done.4.home_c = bf16[7,128,128]{2,1,0:T(8,128)(2,1)S(1)} collective-permute-done((bf16[7,128,128]{2,1,0:T(8,128)(2,1)S(1)}, bf16[7,128,128]{2,1,0:T(8,128)(2,1)S(1)}, u32[]{:S(2)}, u32[]{:S(2)}) %collective-permute-start.4) | collective-permute-done | bytes 229408 | tf_op jit(solution)/shard_map/ppermute | solution.py:248
  99.9 11.9 %collective-permute-done.5.out_c = bf16[8,128,128]{2,1,0:T(8,128)(2,1)S(1)} collective-permute-done((bf16[8,128,128]{2,1,0:T(8,128)(2,1)S(1)}, bf16[8,128,128]{2,1,0:T(8,128)(2,1)S(1)}, u32[]{:S(2)}, u32[]{:S(2)}) %collective-permute-start.5) | collective-permute-done | bytes 262176 | tf_op jit(solution)/shard_map/ppermute | solution.py:258
  111.8 0.1 join.1
  111.9 0.0 all-to-all-done.3.parts_s
  111.9 12.9 %all_to_all.20.parts = bf16[8,3,128,128]{3,2,1,0:T(8,128)(2,1)S(1)} all-to-all(bf16[8,3,128,128]{3,2,1,0:T(8,128)(2,1)S(1)} %join.1), channel_id=1, replica_groups={{0,2,4,6,8,10,12,14},{16,18,20,22,24,26,28,30},{32,34,36,38,40,42,44,46..., dimensions={0} | all-to-all | bytes 1572864 | tf_op jit(solution)/shard_map/all_to_all | solution.py:254
  124.9 1.2 unpack.1
  (2 shorter events, 0.0 us)
Async XLA Ops:
  3.1 17.4 %all-to-all-start = ((bf16[8,3,128,128]{3,2,1,0:T(8,128)(2,1)}), bf16[8,3,128,128]{3,2,1,0:T(8,128)(2,1)S(1)}, u32[]{:S(2)}, u32[]{:S(2)}) async-start(bf16[8,3,128,128]{3,2,1,0:T(8,128)(2,1)} %get-tuple-element.24), calls=%async_computation | async-start | bytes 1572864 | tf_op jit(solution)/shard_map/all_to_all | solution.py:254
  8.5 32.3 %collective-permute-start.1 = (bf16[8,128,128]{2,1,0:T(8,128)(2,1)S(1)}, bf16[8,128,128]{2,1,0:T(8,128)(2,1)}, u32[]{:S(2)}, u32[]{:S(2)}) collective-permute-start(bf16[8,128,128]{2,1,0:T(8,128)(2,1)S(1)} %get-tuple-element.26), channel_id=1, source_target_pairs={{0,256},{256,0},{1,257},{257,1},{2,258},{258,2},{3,259},{259,3},{4... | collective-permute-start | bytes 786440 | tf_op jit(solution)/shard_map/ppermute | solution.py:258
  20.6 30.8 %collective-permute-start.2 = (bf16[7,128,128]{2,1,0:T(8,128)(2,1)S(1)}, bf16[7,128,128]{2,1,0:T(8,128)(2,1)S(1)}, u32[]{:S(2)}, u32[]{:S(2)}) collective-permute-start(bf16[7,128,128]{2,1,0:T(8,128)(2,1)S(1)} %get-tuple-element.41), channel_id=1, source_target_pairs={{0,24},{2,26},{4,28},{6,30},{8,16},{10,18},{12,20},{14,22},{16,40}... | collective-permute-start | bytes 688136 | tf_op jit(solution)/shard_map/ppermute | solution.py:248
  51.3 11.6 %all-to-all-start.1 = ((bf16[8,128,128]{2,1,0:T(8,128)(2,1)}), bf16[8,128,128]{2,1,0:T(8,128)(2,1)S(1)}, u32[]{:S(2)}, u32[]{:S(2)}) async-start(bf16[8,128,128]{2,1,0:T(8,128)(2,1)} %collective-permute-done.1), calls=%async_computation.1 | async-start | bytes 524288 | tf_op jit(solution)/shard_map/all_to_all | solution.py:254
  55.5 14.1 %collective-permute-start = (bf16[7,128,128]{2,1,0:T(8,128)(2,1)S(1)}, bf16[7,128,128]{2,1,0:T(8,128)(2,1)S(1)}, u32[]{:S(2)}, u32[]{:S(2)}) collective-permute-start(bf16[7,128,128]{2,1,0:T(8,128)(2,1)S(1)} %get-tuple-element.42), channel_id=1, source_target_pairs={{0,24},{2,26},{4,28},{6,30},{8,16},{10,18},{12,20},{14,22},{16,40}... | collective-permute-start | bytes 688136 | tf_op jit(solution)/shard_map/ppermute | solution.py:248
  67.8 44.1 %collective-permute-start.5 = (bf16[8,128,128]{2,1,0:T(8,128)(2,1)S(1)}, bf16[8,128,128]{2,1,0:T(8,128)(2,1)S(1)}, u32[]{:S(2)}, u32[]{:S(2)}) collective-permute-start(bf16[8,128,128]{2,1,0:T(8,128)(2,1)S(1)} %get-tuple-element.32), channel_id=1, source_target_pairs={{0,256},{256,0},{1,257},{257,1},{2,258},{258,2},{3,259},{259,3},{4... | collective-permute-start | bytes 786440 | tf_op jit(solution)/shard_map/ppermute | solution.py:258
  75.1 22.1 %collective-permute-start.3 = (bf16[7,128,128]{2,1,0:T(8,128)(2,1)S(1)}, bf16[7,128,128]{2,1,0:T(8,128)(2,1)S(1)}, u32[]{:S(2)}, u32[]{:S(2)}) collective-permute-start(bf16[7,128,128]{2,1,0:T(8,128)(2,1)S(1)} %get-tuple-element.30), channel_id=1, source_target_pairs={{0,248},{2,250},{4,252},{6,254},{8,240},{10,242},{12,244},{14,246}... | collective-permute-start | bytes 688136 | tf_op jit(solution)/shard_map/ppermute | solution.py:248
  87.2 12.7 %collective-permute-start.4 = (bf16[7,128,128]{2,1,0:T(8,128)(2,1)S(1)}, bf16[7,128,128]{2,1,0:T(8,128)(2,1)S(1)}, u32[]{:S(2)}, u32[]{:S(2)}) collective-permute-start(bf16[7,128,128]{2,1,0:T(8,128)(2,1)S(1)} %get-tuple-element.31), channel_id=1, source_target_pairs={{0,248},{2,250},{4,252},{6,254},{8,240},{10,242},{12,244},{14,246}... | collective-permute-start | bytes 688136 | tf_op jit(solution)/shard_map/ppermute | solution.py:248
  89.2 22.7 %all-to-all-start.3 = ((bf16[8,128,128]{2,1,0:T(8,128)(2,1)}), bf16[8,128,128]{2,1,0:T(8,128)(2,1)S(1)}, u32[]{:S(2)}, u32[]{:S(2)}) async-start(bf16[8,128,128]{2,1,0:T(8,128)(2,1)} %get-tuple-element.33), calls=%async_computation.3 | async-start | bytes 524288 | tf_op jit(solution)/shard_map/all_to_all | solution.py:254

commit v7 on v5

--- a/solution.py
+++ b/solution.py
@@ -135,14 +135,16 @@
         )
         out[m] = result.T.astype(jnp.bfloat16)
 
-    def key_side(w):
-        low, high = max(0, w - HALO), min(TEAM - 1, w) + 1
-        total = lax.dot_general(
+    def key_terms(w, low, high):
+        return lax.dot_general(
             probs[w * ROWS : (w + 1) * ROWS, low * BOTH : high * BOTH],
             stacks[low * BOTH : high * BOTH, :],
             (((1,), (0,)), ((), ())),
             preferred_element_type=jnp.float32,
         )
+
+    def key_side(w):
+        total = key_terms(w, max(0, w - HALO), min(TEAM - 1, w) + 1)
         if w < HALO:
             dkv_halo[w] = total.astype(jnp.bfloat16)
         else:
@@ -160,6 +162,8 @@
             raise_up(m, k, top)
             if m + 1 < TEAM:
                 score(m + 1, k)
+            elif k < HALO - 1:
+                dkv_own[k + 1] = key_terms(TEAM + k, k + 1, TEAM - 1)
         if m + 1 < TEAM:
             turn(m + GROUP)
         scale = 1.0 / jnp.sum(sums[m][0], axis=0, keepdims=True)
@@ -171,8 +175,10 @@
             if m and k == 4:
                 key_side(m - 1)
     query_side(TEAM - 1)
-    for w in range(TEAM - 1, HALO + TEAM):
-        key_side(w)
+    key_side(TEAM - 1)
+    for b in range(1, TEAM - 1):
+        dkv_own[b] += key_terms(b + HALO, TEAM - 1, TEAM)
+    key_side(HALO + TEAM - 1)
 
 
 def attention(kind, *operands):

time: 123 us -> 123 us (level)
  transfers between devices with their start and end apart: 8 -> 8, of which waited for: 5 -> 5; matrix products, arithmetic and copies ran while one was open for 0% -> 0% of each run, Pallas kernels for 5% -> 4%
where the time goes in v7:
time: 123 us
  starting transfers between devices  54.3 us (44%)
  waiting for transfers between devices  31.5 us (26%)
  blocking collectives  21.5 us (17%)
  Pallas kernels  13.9 us (11%)
  between operations  1.39 us (1%)
    ppermute x2, starting transfers between devices, swapped(): return lax.ppermute(value, 'tower', [(0, 1), (1, 0)])  26.6 us
    all_to_all x1, blocking collectives, within_team(): lax.all_to_all(value, 'ctx', 0, 0, axis_index_groups=teams, tiled=True)  21.5 us
    ppermute x3, waiting for transfers between devices, to_next_team(): return lax.ppermute(value, 'ctx', route)  15 us
    all_to_all x3, starting transfers between devices, within_team(): lax.all_to_all(value, 'ctx', 0, 0, axis_index_groups=teams, tiled=True)  14.3 us
    ppermute x3, starting transfers between devices, to_next_team(): return lax.ppermute(value, 'ctx', route)  13.4 us
    pallas_call x2, Pallas kernels, attention(): pl.pallas_call(kernel, out_shape=(block_shape(TEAM), block_shape(TEAM, dt...  10.2 us
    ppermute x2, waiting for transfers between devices, swapped(): return lax.ppermute(value, 'tower', [(0, 1), (1, 0)])  9.98 us
    all_to_all x3, waiting for transfers between devices, within_team(): lax.all_to_all(value, 'ctx', 0, 0, axis_index_groups=teams, tiled=True)  6.49 us
  transfers between devices with their start and end apart: 8, of which 5 were waited for; matrix products, arithmetic and copies ran while one was open for 0% of the time, Pallas kernels for 4%

profile of v7, /device:TPU:64, one launch (start us, length us, event | category | flops | bytes accessed | tf_op | source)
XLA Modules:
  0.0 122.7 jit_solution(5453913449644213722)
XLA Ops:
  0.6 2.5 %pack.1 = (bf16[8,128,128]{2,1,0:T(8,128)(2,1)S(1)}, bf16[8,3,128,128]{3,2,1,0:T(8,128)(2,1)}) custom-call(bf16[128,512]{1,0:T(8,128)(2,1)} %bitcast.17, bf16[128,512]{1,0:T(8,128)(2,1)} %bitcast.18, bf16[128,512]{1,0:T(8,128)(2,1)} %bitcast.19, bf16[128,512]{1,0:T(8,128)(2,1)} %bitcast.20, bf16[128,512]{1,0:T(8,128)(2,1)} %bitcast.21, ...), custom_call_target="tpu_custom_call" | custom-call | tf_op jit(solution)/shard_map/pack/pallas_call | solution.py:239
  3.1 5.4 %all-to-all-start = ((bf16[8,3,128,128]{3,2,1,0:T(8,128)(2,1)}), bf16[8,3,128,128]{3,2,1,0:T(8,128)(2,1)S(1)}, u32[]{:S(2)}, u32[]{:S(2)}) async-start(bf16[8,3,128,128]{3,2,1,0:T(8,128)(2,1)} %get-tuple-element.22), calls=%async_computation | async-start | bytes 1572864 | tf_op jit(solution)/shard_map/all_to_all | solution.py:260
  8.5 13.9 %collective-permute-start.1 = (bf16[8,128,128]{2,1,0:T(8,128)(2,1)S(1)}, bf16[8,128,128]{2,1,0:T(8,128)(2,1)}, u32[]{:S(2)}, u32[]{:S(2)}) collective-permute-start(bf16[8,128,128]{2,1,0:T(8,128)(2,1)S(1)} %get-tuple-element.24), channel_id=1, source_target_pairs={{0,256},{256,0},{1,257},{257,1},{2,258},{258,2},{3,259},{259,3},{4... | collective-permute-start | bytes 786440 | tf_op jit(solution)/shard_map/ppermute | solution.py:264
  22.5 0.0 all-to-all-done.refs_1_.refs_2_
  22.5 5.2 %collective-permute-start = (bf16[7,2,128,128]{3,2,1,0:T(8,128)(2,1)S(1)}, bf16[7,2,128,128]{3,2,1,0:T(8,128)(2,1)S(1)}, u32[]{:S(2)}, u32[]{:S(2)}) collective-permute-start(bf16[7,2,128,128]{3,2,1,0:T(8,128)(2,1)S(1)} %slice.4), channel_id=1, source_target_pairs={{0,24},{2,26},{4,28},{6,30},{8,16},{10,18},{12,20},{14,22},{16,40}... | collective-permute-start | bytes 1376264 | tf_op jit(solution)/shard_map/ppermute | solution.py:254
  27.7 10.0 %collective-permute-done.1 = bf16[8,128,128]{2,1,0:T(8,128)(2,1)} collective-permute-done((bf16[8,128,128]{2,1,0:T(8,128)(2,1)S(1)}, bf16[8,128,128]{2,1,0:T(8,128)(2,1)}, u32[]{:S(2)}, u32[]{:S(2)}) %collective-permute-start.1) | collective-permute-done | bytes 262176 | tf_op jit(solution)/shard_map/ppermute | solution.py:264
  37.7 5.4 %all-to-all-start.1 = ((bf16[8,128,128]{2,1,0:T(8,128)(2,1)}), bf16[8,128,128]{2,1,0:T(8,128)(2,1)S(1)}, u32[]{:S(2)}, u32[]{:S(2)}) async-start(bf16[8,128,128]{2,1,0:T(8,128)(2,1)} %collective-permute-done.1), calls=%async_computation.1 | async-start | bytes 524288 | tf_op jit(solution)/shard_map/all_to_all | solution.py:260
  43.8 0.1 pad_add_fusion.refs_0_
  43.9 6.5 %all-to-all-done.1.refs_1_ = bf16[8,128,128]{2,1,0:T(8,128)(2,1)S(1)} async-done(((bf16[8,128,128]{2,1,0:T(8,128)(2,1)}), bf16[8,128,128]{2,1,0:T(8,128)(2,1)S(1)}, u32[]{:S(2)}, u32[]{:S(2)}) %all-to-all-start.1) | async-done | bytes 262176 | tf_op jit(solution)/shard_map/all_to_all | solution.py:260
  50.3 6.7 %collective-permute-done.refs_2_.refs_3_ = bf16[7,2,128,128]{3,2,1,0:T(8,128)(2,1)S(1)} collective-permute-done((bf16[7,2,128,128]{3,2,1,0:T(8,128)(2,1)S(1)}, bf16[7,2,128,128]{3,2,1,0:T(8,128)(2,1)S(1)}, u32[]{:S(2)}, u32[]{:S(2)}) %collective-permute-start) | collective-permute-done | bytes 458784 | tf_op jit(solution)/shard_map/ppermute | solution.py:254
  57.0 4.8 %attention_cross.1 = (bf16[8,128,128]{2,1,0:T(8,128)(2,1)S(1)}, f32[8,128,128]{2,1,0:T(8,128)S(1)}, bf16[7,128,128]{2,1,0:T(8,128)(2,1)S(1)}) custom-call(s32[2]{0:T(128)S(1)} %pad_add_fusion.refs_0_, bf16[8,128,128]{2,1,0:T(8,128)(2,1)S(1)} %all-to-all-done.1.refs_1_, bf16[8,3,128,128]{3,2,1,0:T(8,128)(2,1)S(1)} %all-to-all-done.refs_1_.refs_2_, ...), custom_call_target="tpu_custom_call" | custom-call | tf_op jit(solution)/shard_map/attention_cross/pallas_call | solution.py:188
  61.8 12.7 %collective-permute-start.4 = (bf16[8,128,128]{2,1,0:T(8,128)(2,1)S(1)}, bf16[8,128,128]{2,1,0:T(8,128)(2,1)S(1)}, u32[]{:S(2)}, u32[]{:S(2)}) collective-permute-start(bf16[8,128,128]{2,1,0:T(8,128)(2,1)S(1)} %get-tuple-element.28), channel_id=1, source_target_pairs={{0,256},{256,0},{1,257},{257,1},{2,258},{258,2},{3,259},{259,3},{4... | collective-permute-start | bytes 786440 | tf_op jit(solution)/shard_map/ppermute | solution.py:264
  74.5 5.8 %collective-permute-start.3 = (bf16[7,128,128]{2,1,0:T(8,128)(2,1)S(1)}, bf16[7,128,128]{2,1,0:T(8,128)(2,1)S(1)}, u32[]{:S(2)}, u32[]{:S(2)}) collective-permute-start(bf16[7,128,128]{2,1,0:T(8,128)(2,1)S(1)} %get-tuple-element.27), channel_id=1, source_target_pairs={{0,248},{2,250},{4,252},{6,254},{8,240},{10,242},{12,244},{14,246}... | collective-permute-start | bytes 688136 | tf_op jit(solution)/shard_map/ppermute | solution.py:254
  80.3 5.4 %attention_self.1 = (bf16[8,128,128]{2,1,0:T(8,128)(2,1)}, f32[8,128,128]{2,1,0:T(8,128)S(1)}, bf16[7,128,128]{2,1,0:T(8,128)(2,1)}) custom-call(s32[2]{0:T(128)S(1)} %pad_add_fusion.refs_0_, bf16[8,3,128,128]{3,2,1,0:T(8,128)(2,1)S(1)} %all-to-all-done.refs_1_.refs_2_, bf16[7,2,128,128]{3,2,1,0:T(8,128)(2,1)S(1)} %collective-permute-done.refs_2_.refs_3_), custom_call_target="tpu_custom_call" | custom-call | tf_op jit(solution)/shard_map/attention_self/pallas_call | solution.py:188
  85.7 2.4 %collective-permute-start.2 = (bf16[7,128,128]{2,1,0:T(8,128)(2,1)}, bf16[7,128,128]{2,1,0:T(8,128)(2,1)S(1)}, u32[]{:S(2)}, u32[]{:S(2)}) collective-permute-start(bf16[7,128,128]{2,1,0:T(8,128)(2,1)} %get-tuple-element.26), channel_id=1, source_target_pairs={{0,248},{2,250},{4,252},{6,254},{8,240},{10,242},{12,244},{14,246}... | collective-permute-start | bytes 688136 | tf_op jit(solution)/shard_map/ppermute | solution.py:254
  88.1 3.4 %all-to-all-start.3 = ((bf16[8,128,128]{2,1,0:T(8,128)(2,1)}), bf16[8,128,128]{2,1,0:T(8,128)(2,1)S(1)}, u32[]{:S(2)}, u32[]{:S(2)}) async-start(bf16[8,128,128]{2,1,0:T(8,128)(2,1)} %get-tuple-element.29), calls=%async_computation.3 | async-start | bytes 524288 | tf_op jit(solution)/shard_map/all_to_all | solution.py:260
  91.6 3.8 %collective-permute-done.3.home_c = bf16[7,128,128]{2,1,0:T(8,128)(2,1)S(1)} collective-permute-done((bf16[7,128,128]{2,1,0:T(8,128)(2,1)S(1)}, bf16[7,128,128]{2,1,0:T(8,128)(2,1)S(1)}, u32[]{:S(2)}, u32[]{:S(2)}) %collective-permute-start.3) | collective-permute-done | bytes 229408 | tf_op jit(solution)/shard_map/ppermute | solution.py:254
  95.4 4.5 %collective-permute-done.2.home_s = bf16[7,128,128]{2,1,0:T(8,128)(2,1)S(1)} collective-permute-done((bf16[7,128,128]{2,1,0:T(8,128)(2,1)}, bf16[7,128,128]{2,1,0:T(8,128)(2,1)S(1)}, u32[]{:S(2)}, u32[]{:S(2)}) %collective-permute-start.2) | collective-permute-done | bytes 229408 | tf_op jit(solution)/shard_map/ppermute | solution.py:254
  99.9 0.0 collective-permute-done.4.out_c
  99.9 0.1 join.1
  100.0 0.0 all-to-all-done.3.parts_s
  100.0 21.5 %all_to_all.20.parts = bf16[8,3,128,128]{3,2,1,0:T(8,128)(2,1)S(1)} all-to-all(bf16[8,3,128,128]{3,2,1,0:T(8,128)(2,1)S(1)} %join.1), channel_id=1, replica_groups={{0,2,4,6,8,10,12,14},{16,18,20,22,24,26,28,30},{32,34,36,38,40,42,44,46..., dimensions={0} | all-to-all | bytes 1572864 | tf_op jit(solution)/shard_map/all_to_all | solution.py:260
  121.5 1.2 unpack.1
  (1 shorter events, 0.0 us)
Async XLA Ops:
  3.1 19.3 %all-to-all-start = ((bf16[8,3,128,128]{3,2,1,0:T(8,128)(2,1)}), bf16[8,3,128,128]{3,2,1,0:T(8,128)(2,1)S(1)}, u32[]{:S(2)}, u32[]{:S(2)}) async-start(bf16[8,3,128,128]{3,2,1,0:T(8,128)(2,1)} %get-tuple-element.22), calls=%async_computation | async-start | bytes 1572864 | tf_op jit(solution)/shard_map/all_to_all | solution.py:260
  8.5 29.2 %collective-permute-start.1 = (bf16[8,128,128]{2,1,0:T(8,128)(2,1)S(1)}, bf16[8,128,128]{2,1,0:T(8,128)(2,1)}, u32[]{:S(2)}, u32[]{:S(2)}) collective-permute-start(bf16[8,128,128]{2,1,0:T(8,128)(2,1)S(1)} %get-tuple-element.24), channel_id=1, source_target_pairs={{0,256},{256,0},{1,257},{257,1},{2,258},{258,2},{3,259},{259,3},{4... | collective-permute-start | bytes 786440 | tf_op jit(solution)/shard_map/ppermute | solution.py:264
  22.5 34.5 %collective-permute-start = (bf16[7,2,128,128]{3,2,1,0:T(8,128)(2,1)S(1)}, bf16[7,2,128,128]{3,2,1,0:T(8,128)(2,1)S(1)}, u32[]{:S(2)}, u32[]{:S(2)}) collective-permute-start(bf16[7,2,128,128]{3,2,1,0:T(8,128)(2,1)S(1)} %slice.4), channel_id=1, source_target_pairs={{0,24},{2,26},{4,28},{6,30},{8,16},{10,18},{12,20},{14,22},{16,40}... | collective-permute-start | bytes 1376264 | tf_op jit(solution)/shard_map/ppermute | solution.py:254
  37.7 12.6 %all-to-all-start.1 = ((bf16[8,128,128]{2,1,0:T(8,128)(2,1)}), bf16[8,128,128]{2,1,0:T(8,128)(2,1)S(1)}, u32[]{:S(2)}, u32[]{:S(2)}) async-start(bf16[8,128,128]{2,1,0:T(8,128)(2,1)} %collective-permute-done.1), calls=%async_computation.1 | async-start | bytes 524288 | tf_op jit(solution)/shard_map/all_to_all | solution.py:260
  61.8 38.2 %collective-permute-start.4 = (bf16[8,128,128]{2,1,0:T(8,128)(2,1)S(1)}, bf16[8,128,128]{2,1,0:T(8,128)(2,1)S(1)}, u32[]{:S(2)}, u32[]{:S(2)}) collective-permute-start(bf16[8,128,128]{2,1,0:T(8,128)(2,1)S(1)} %get-tuple-element.28), channel_id=1, source_target_pairs={{0,256},{256,0},{1,257},{257,1},{2,258},{258,2},{3,259},{259,3},{4... | collective-permute-start | bytes 786440 | tf_op jit(solution)/shard_map/ppermute | solution.py:264
  74.5 20.9 %collective-permute-start.3 = (bf16[7,128,128]{2,1,0:T(8,128)(2,1)S(1)}, bf16[7,128,128]{2,1,0:T(8,128)(2,1)S(1)}, u32[]{:S(2)}, u32[]{:S(2)}) collective-permute-start(bf16[7,128,128]{2,1,0:T(8,128)(2,1)S(1)} %get-tuple-element.27), channel_id=1, source_target_pairs={{0,248},{2,250},{4,252},{6,254},{8,240},{10,242},{12,244},{14,246}... | collective-permute-start | bytes 688136 | tf_op jit(solution)/shard_map/ppermute | solution.py:254
  85.7 14.3 %collective-permute-start.2 = (bf16[7,128,128]{2,1,0:T(8,128)(2,1)}, bf16[7,128,128]{2,1,0:T(8,128)(2,1)S(1)}, u32[]{:S(2)}, u32[]{:S(2)}) collective-permute-start(bf16[7,128,128]{2,1,0:T(8,128)(2,1)} %get-tuple-element.26), channel_id=1, source_target_pairs={{0,248},{2,250},{4,252},{6,254},{8,240},{10,242},{12,244},{14,246}... | collective-permute-start | bytes 688136 | tf_op jit(solution)/shard_map/ppermute | solution.py:254
  88.1 11.9 %all-to-all-start.3 = ((bf16[8,128,128]{2,1,0:T(8,128)(2,1)}), bf16[8,128,128]{2,1,0:T(8,128)(2,1)S(1)}, u32[]{:S(2)}, u32[]{:S(2)}) async-start(bf16[8,128,128]{2,1,0:T(8,128)(2,1)} %get-tuple-element.29), calls=%async_computation.3 | async-start | bytes 524288 | tf_op jit(solution)/shard_map/all_to_all | solution.py:260
